TPU v7x, 512 devices: a whole 4x4x16 slice. The times are simulated.
512 devices in a mesh: stream: 64 (over x, z_lo, core), span: 8 (over z_hi, y).
Axes of the slice: x: 4, y: 4, z: 16 (z_hi: 2, z_lo: 8; z = z_hi * 8 + z_lo), core: 2. Of those that a mesh axis runs over, the one named last changes fastest.
Arguments:
- adjoint: float32 [7, 384, 64, 1152], P(None, 'stream', 'span'), may hold values from -6 to 6
- source: bfloat16 [7, 384, 64, 1152], P(None, 'stream', 'span'), may hold values from -6 to 6
- stencil: float32 [384, 64, 768], P('stream', 'span'), may hold values from 0.1 to 0.4
- line_coupling: float32 [6, 192], replicated, may hold values from 0.5 to 2
- line_diag: float32 [6, 192], replicated, may hold values from 0.0005 to 4
- omega: float32 [1], replicated, may hold values from 0.1 to 0.4
- phase: float32 [1], replicated, may hold values from -3.140625 to 3.140625
- match_owner: int32 [64, 8, 48, 1], P('stream', 'span'), may hold values from 0 to 63, as said below
- match_row: int32 [64, 8, 48], P('stream', 'span'), may hold values from 0 to 47
- tile_live: int32 [64, 8], P('stream', 'span'), may hold values from 12 to 48
Outputs:
- updated: float32 [7, 384, 64, 1152], P(None, 'stream', 'span')
Inputs may be any that keep to these rules, and one draw needn't show every extreme that they name: `match_owner`: for tile (i, j), every owner is (i + 32 + o) mod 64 with o from -3 to 4; in the lines of one tile no owner is named by more than 8 lines, and one owner is named by exactly 8.
All inputs are finite; a program needn't handle non-finite values.
Results may differ from a plain program's by a relative error of at most 0.0008.
Values may be sent and summed in bfloat16 or wider, within the bound.
No kernel may reach another device: no remote copies, remote signals or barrier semaphores. Data moves between devices by JAX's collectives and lax.ppermute only.
A program may use at most 128 MiB of HBM per device.

v0:
```python
import functools
import math

import jax
import jax.numpy as jnp
from jax import lax
from jax.experimental import pallas as pl
from jax.experimental.pallas import tpu as pltpu
from jax.sharding import PartitionSpec as P

F32 = jnp.float32
BF16 = jnp.bfloat16
LANES = 128
HALF = 64
REACH = 3
OWNERS = 8


def iota(shape, dim):
    return lax.broadcasted_iota(jnp.int32, shape, dim)


def split(value):
    high = value.astype(BF16)
    return high, (value - high.astype(F32)).astype(BF16)


def edge_kernel(dims, u_ref, west_ref, east_ref, south_ref, north_ref, rim_ref):
    times, cx, cz, pairs = dims
    rows = cx * cz
    width = u_ref.shape[1]
    take = lambda t, x: u_ref[t * rows + x * cz : t * rows + x * cz + cz, :]
    west_ref[...] = jnp.concatenate([take(t, 0) for t in range(times)], 0).astype(BF16)
    east_ref[...] = jnp.concatenate([take(t, cx - 1) for t in range(times)], 0).astype(BF16)
    sub = iota((8, width), 0)
    for ref, z in ((south_ref, 0), (north_ref, cz - 1)):
        tiles = []
        for x in range(cx):
            tile = jnp.zeros((8, width), F32)
            for t in range(times):
                at = t * rows + x * cz + z
                tile = jnp.where(sub == t, u_ref[at : at + 1, :], tile)
            tiles.append(tile)
        ref[...] = jnp.concatenate(tiles, 0).astype(BF16)
    lane = iota((rows, LANES), 1)
    inner = lane % HALF
    found = jnp.zeros((rows, LANES), F32)
    for t in range(times):
        for pair in range(pairs):
            base = pair * 3 * LANES
            block = slice(t * rows, (t + 1) * rows)
            first = u_ref[block, base + LANES : base + 2 * LANES]
            second = u_ref[block, base + 2 * LANES : base + 3 * LANES]
            both = jnp.where(lane < HALF, first, second)
            spot = t * pairs + pair
            both = pltpu.roll(both, (spot - (HALF - 1)) % LANES, 1)
            found = jnp.where(inner == spot, both, found)
    high = found.astype(BF16).astype(F32)
    rest = found - high
    middle = rest.astype(BF16).astype(F32)
    low = rest - middle
    span = times * pairs
    rim = high + pltpu.roll(middle, span, 1) + pltpu.roll(low, 2 * span, 1)
    rim_ref[...] = rim.astype(BF16)


def scan_products(matrix, lane, points, backward):
    a, b, c, d = matrix
    step = 1
    while step < points:
        shift = (lane.shape[1] - step) if backward else step
        inside = (lane < points - step) if backward else (lane >= step)
        e = jnp.where(inside, pltpu.roll(a, shift, 1), 1.0)
        f = jnp.where(inside, pltpu.roll(b, shift, 1), 0.0)
        g = jnp.where(inside, pltpu.roll(c, shift, 1), 0.0)
        h = jnp.where(inside, pltpu.roll(d, shift, 1), 1.0)
        a, b, c, d = a * e + b * g, a * f + b * h, c * e + d * g, c * f + d * h
        scale = 1.0 / (a + b + c + d)
        a, b, c, d = a * scale, b * scale, c * scale, d * scale
        step *= 2
    return a / c


def local_kernel(
    dims,
    omega_ref,
    phase_ref,
    live_ref,
    place_ref,
    u_ref,
    source_ref,
    stencil_ref,
    coupling_ref,
    diag_ref,
    owner_ref,
    row_ref,
    work_ref,
    green_ref,
    shift_ref,
    pick_ref,
    rimw_ref,
    couple_s,
    diag_s,
    green_row,
    sum_row,
    green_col,
    sum_col,
    face_s,
    round_s,
):
    times, cx, cz, pairs, points, count = dims
    rows = cx * cz
    span = times * pairs
    pair_now = pl.program_id(0)
    wide = couple_s.shape[1]

    @pl.when(pair_now == 0)
    def prepare():
        states = coupling_ref.shape[0]
        lane = iota((8, wide), 1)
        couple_s[...] = jnp.ones_like(couple_s)
        diag_s[...] = jnp.ones_like(diag_s)
        couple_s[0:states, 0:points] = coupling_ref[...]
        diag_s[0:states, 0:points] = diag_ref[...]
        link = couple_s[...]
        diag = diag_s[...]
        before = jnp.where(lane == 0, 0.0, pltpu.roll(link, 1, 1))
        one = jnp.ones_like(link)
        e = scan_products((diag + before, diag * before, one, before), lane, points, False)
        inside = lane < points
        matrix = (
            jnp.where(inside, diag + link, 1.0),
            jnp.where(inside, diag * link, 0.0),
            jnp.where(inside, one, 0.0),
            jnp.where(inside, link, 1.0),
        )
        f = jnp.where(inside, scan_products(matrix, lane, points, True), 1.0)
        e_before = jnp.where(lane == 0, 1.0, pltpu.roll(e, 1, 1))
        e_before = jnp.where(inside, e_before, 1.0)
        green = 1.0 / (before * e_before / (before + e_before) + f)
        decay = jnp.log(1.0 + f / jnp.where(lane == 0, 1.0, before))
        decay = jnp.where((lane == 0) | (lane >= points), 0.0, decay)
        step = 1
        while step < points:
            decay = decay + jnp.where(lane >= step, pltpu.roll(decay, step, 1), 0.0)
            step *= 2
        odd = iota((8, wide), 0) % 2 == 1
        green = jnp.where(odd, pltpu.roll(green, HALF, 1), green)
        decay = jnp.where(odd, pltpu.roll(decay, HALF, 1), decay)
        green_row[...] = green
        sum_row[...] = decay
        green_col[...] = green.T
        sum_col[...] = decay.T

        low = iota((rows, LANES), 1) < HALF
        z = iota((rows, 3 * LANES), 0) % cz
        for way in range(4):
            at = way // 2 * 3 * LANES
            t0, t1, t2 = (stencil_ref[:, at + k * LANES : at + (k + 1) * LANES] for k in range(3))
            if way % 2 == 0:
                swap = pltpu.roll(t0, HALF, 1)
                tiles = (t0, jnp.where(low, t1, swap), jnp.where(low, swap, pltpu.roll(t1, HALF, 1)))
            else:
                swap = pltpu.roll(t2, HALF, 1)
                other = pltpu.roll(t1, HALF, 1)
                tiles = (jnp.where(low, other, swap), jnp.where(low, swap, t1), t2)
            face = jnp.concatenate(tiles, 1)
            if way == 0:
                rimw_ref[0:cz, :] = face[0:cz]
            elif way == 1:
                rimw_ref[cz : 2 * cz, :] = face[rows - cz :]
            elif way == 2:
                rimw_ref[2 * cz : 2 * cz + rows, :] = jnp.where(z == 0, face, 0.0)
                face = jnp.where(z == 0, 0.0, face)
            else:
                rimw_ref[2 * cz + rows : 2 * cz + 2 * rows, :] = jnp.where(z == cz - 1, face, 0.0)
                face = jnp.where(z == cz - 1, 0.0, face)
            face_s[way * rows : (way + 1) * rows, :] = face

        slot = owner_ref[...] - place_ref[0] + (count // 2 + REACH)
        slot = jnp.where(slot < 0, slot + count, slot)
        slot = jnp.where(slot >= count, slot - count, slot)
        diagonal = iota((rows, rows), 0) == iota((rows, rows), 1)
        target = jnp.sum(jnp.where(diagonal, row_ref[...].astype(F32), 0.0), axis=1, keepdims=True)
        target = target.astype(jnp.int32)
        wanted = slot * rows + target
        cell = iota((rows, OWNERS * rows), 1)
        pick_ref[...] = jnp.where(cell == wanted, 1.0, 0.0).astype(BF16)

        left = iota((LANES, LANES), 0)
        right = iota((LANES, LANES), 1)
        left_in = left % HALF
        right_in = right % HALF
        left_in_part = left_in % span
        offset = right_in // pairs - left_in_part // pairs
        angle = (2.0 * math.pi / times) * offset.astype(F32)
        total = jnp.ones((LANES, LANES), F32)
        for harmonic in range(1, (times - 1) // 2 + 1):
            total = total + 2.0 * jnp.cos(harmonic * (angle + phase_ref[0]))
        ok = (left // HALF != right // HALF) & (left_in_part % pairs == right_in % pairs)
        ok = ok & (right_in < span) & (left_in < 3 * span)
        high, low_part = split(jnp.where(ok, total / times, 0.0))
        shift_ref[0:LANES, :] = high
        shift_ref[LANES : 2 * LANES, :] = low_part

    for half in range(2):
        state = 2 * pair_now + half
        first = half * HALF
        g_row = green_row[pl.ds(state, 1), :]
        s_row = sum_row[pl.ds(state, 1), :]
        pick = iota((wide, 8), 1) == state
        g_col = jnp.sum(jnp.where(pick, green_col[...], 0.0), axis=1, keepdims=True)
        s_col = jnp.sum(jnp.where(pick, sum_col[...], 0.0), axis=1, keepdims=True)
        k = iota((wide, wide), 0)
        n = iota((wide, wide), 1)
        full = jnp.exp(-jnp.abs(s_col - s_row)) * jnp.where(k <= n, g_col, g_row)
        at_end = first + points - 1
        lane = iota((1, wide), 1)
        s_end = jnp.sum(jnp.where(lane == at_end, s_row, 0.0), axis=1, keepdims=True)
        link = couple_s[pl.ds(state, 1), :]
        c_end = jnp.sum(jnp.where(lane == points - 1, link, 0.0), axis=1, keepdims=True)
        last = c_end * jnp.exp(-jnp.abs(s_end - s_row)) * g_row
        inside_k = (k >= first) & (k < first + points)
        inside_n = (n >= first) & (n < first + points)
        inner = k % HALF
        added = (inner < span) & (inner % pairs == pair_now)
        full = jnp.where(inside_k, full, jnp.where(added, last, 0.0))
        full = jnp.where(inside_n, full, 0.0)
        high, low_part = split(full)
        green_ref[0, 2 * half] = high
        green_ref[0, 2 * half + 1] = low_part

    round_s[...] = u_ref[...].astype(BF16).astype(F32)
    omega = omega_ref[0]
    live = live_ref[0]
    z = iota((cz, 3 * LANES), 0)
    weights = []
    for n in range(1, (times - 1) // 2 + 1):
        weights.append(omega * (0.5 * (-1.0) ** n / math.sin(math.pi * n / times)))
    for x in range(cx):
        west, east, south, north = (
            face_s[way * rows + x * cz : way * rows + (x + 1) * cz, :] for way in range(4)
        )
        for t in range(times):
            at = lambda tt, xx: slice((tt % times) * rows + xx * cz, (tt % times) * rows + (xx + 1) * cz)
            here = round_s[at(t, x), :]
            value = source_ref[t, x].astype(F32)
            value += south * pltpu.roll(here, 1, 0) + north * pltpu.roll(here, cz - 1, 0)
            if x > 0:
                value += west * round_s[at(t, x - 1), :]
            if x < cx - 1:
                value += east * round_s[at(t, x + 1), :]
            for n, weight in enumerate(weights, 1):
                value -= weight * (u_ref[at(t + n, x), :] - u_ref[at(t - n, x), :])
            work_ref[at(t, x), :] = jnp.where(z + x * cz < live, value, u_ref[at(t, x), :])


def finish_kernel(dims, groups, live_ref, *refs):
    times, cx, cz, pairs, points = dims
    rim_refs = refs[:groups]
    (
        work_ref,
        green_ref,
        shift_ref,
        pick_ref,
        rimw_ref,
        west_ref,
        east_ref,
        south_ref,
        north_ref,
        out_ref,
        rim_s,
        ghost_s,
        south_s,
        north_s,
        high_s,
        low_s,
    ) = refs[groups:]
    rows = cx * cz

    @pl.when(pl.program_id(0) == 0)
    def ghosts():
        at = 0
        for ref in rim_refs:
            rim_s[at : at + ref.shape[0], :] = ref[...]
            at += ref.shape[0]
        picked = jnp.dot(pick_ref[...], rim_s[...], preferred_element_type=F32).astype(BF16)
        ghost = jnp.dot(picked, shift_ref[0:LANES, :], preferred_element_type=F32)
        ghost += jnp.dot(picked, shift_ref[LANES : 2 * LANES, :], preferred_element_type=F32)
        ghost_s[...] = ghost

    west = west_ref[...].astype(F32)
    east = east_ref[...].astype(F32)
    south_s[...] = south_ref[...].astype(F32)
    north_s[...] = north_ref[...].astype(F32)
    lane = iota((cz, LANES), 1)
    inner = lane % HALF
    low_half = lane < HALF
    for t in range(times):
        mine = (inner >= t * pairs) & (inner < (t + 1) * pairs)
        even, odd = [], []
        for x in range(cx):
            at = t * rows + x * cz
            value = work_ref[at : at + cz, :]
            if x == 0:
                value += rimw_ref[0:cz, :] * west[t * cz : (t + 1) * cz]
            if x == cx - 1:
                value += rimw_ref[cz : 2 * cz, :] * east[t * cz : (t + 1) * cz]
            south = rimw_ref[2 * cz + x * cz : 2 * cz + (x + 1) * cz, :]
            north = rimw_ref[2 * cz + rows + x * cz : 2 * cz + rows + (x + 1) * cz, :]
            value += south * south_s[x * 8 + t : x * 8 + t + 1, :]
            value += north * north_s[x * 8 + t : x * 8 + t + 1, :]
            ghost = jnp.where(mine, ghost_s[x * cz : (x + 1) * cz, :], 0.0)
            mid = value[:, LANES : 2 * LANES]
            even.append(jnp.concatenate([value[:, :LANES], jnp.where(low_half, mid, ghost)], 1))
            odd.append(jnp.concatenate([jnp.where(low_half, ghost, mid), value[:, 2 * LANES :]], 1))
        for half, pieces in ((0, even), (1, odd)):
            high, low = split(jnp.concatenate(pieces, 0))
            high_s[half, t * rows : (t + 1) * rows, :] = high
            low_s[half, t * rows : (t + 1) * rows, :] = low
    products = []
    for half in range(2):
        high = high_s[half]
        g_high = green_ref[0, 2 * half]
        total = jnp.dot(high, g_high, preferred_element_type=F32)
        total += jnp.dot(high, green_ref[0, 2 * half + 1], preferred_element_type=F32)
        total += jnp.dot(low_s[half], g_high, preferred_element_type=F32)
        products.append(total)
    even, odd = products
    tiles = (even[:, :LANES], even[:, LANES:] + odd[:, :LANES], odd[:, LANES:])
    live = live_ref[0]
    shape = out_ref.shape[:1] + (LANES,)
    alive = iota(shape, 0) % rows < live
    for k, tile in enumerate(tiles):
        lanes = slice(k * LANES, (k + 1) * LANES)
        out_ref[:, lanes] = jnp.where(alive, tile, work_ref[:, lanes])


def around(count, offset):
    return [((i + offset) % count, i) for i in range(count)]


def body(
    adjoint,
    source,
    stencil,
    line_coupling,
    line_diag,
    omega,
    phase,
    match_owner,
    match_row,
    tile_live,
):
    times, cx, cz, width = adjoint.shape
    states, points = line_coupling.shape
    pairs = states // 2
    rows = cx * cz
    lines = times * rows
    count = lax.axis_size("stream")
    spans = lax.axis_size("span")
    wide = 2 * LANES
    u = adjoint.reshape(lines, width)
    vmem = pl.BlockSpec(memory_space=pltpu.VMEM)
    smem = pl.BlockSpec(memory_space=pltpu.SMEM)
    west, east, south, north, rim = pl.pallas_call(
        functools.partial(edge_kernel, (times, cx, cz, pairs)),
        out_shape=(
            jax.ShapeDtypeStruct((times * cz, width), BF16),
            jax.ShapeDtypeStruct((times * cz, width), BF16),
            jax.ShapeDtypeStruct((cx * 8, width), BF16),
            jax.ShapeDtypeStruct((cx * 8, width), BF16),
            jax.ShapeDtypeStruct((rows, LANES), BF16),
        ),
        in_specs=[vmem],
        out_specs=(vmem,) * 5,
        name="edges",
    )(u)

    up = [(i, i + 1) for i in range(count - 1)]
    down = [(i + 1, i) for i in range(count - 1)]
    span_up = [(i, i + 1) for i in range(spans - 1)]
    span_down = [(i + 1, i) for i in range(spans - 1)]
    rim_two = jnp.concatenate([rim, lax.ppermute(rim, "stream", around(count, 1))], 0)
    far = [
        lax.ppermute(rim_two, "stream", around(count, count // 2 + offset))
        for offset in range(-REACH, OWNERS - REACH, 2)
    ]
    from_west = lax.ppermute(east, "stream", up)
    from_east = lax.ppermute(west, "stream", down)
    from_south = lax.ppermute(north, "span", span_up)
    from_north = lax.ppermute(south, "span", span_down)

    live = tile_live.reshape(1)
    place = lax.axis_index("stream").astype(jnp.int32).reshape(1)
    trio = 3 * LANES
    rim_rows = 2 * cz + 2 * rows
    work, green, shift, pick, rim_weights = pl.pallas_call(
        functools.partial(local_kernel, (times, cx, cz, pairs, points, count)),
        out_shape=(
            jax.ShapeDtypeStruct((lines, width), F32),
            jax.ShapeDtypeStruct((pairs, 4, wide, wide), BF16),
            jax.ShapeDtypeStruct((2 * LANES, LANES), BF16),
            jax.ShapeDtypeStruct((rows, OWNERS * rows), BF16),
            jax.ShapeDtypeStruct((rim_rows, trio), F32),
        ),
        grid=(pairs,),
        in_specs=[
            smem,
            smem,
            smem,
            smem,
            pl.BlockSpec((lines, trio), lambda p: (0, p)),
            pl.BlockSpec((times, cx, cz, trio), lambda p: (0, 0, 0, p)),
            pl.BlockSpec((rows, 4 * points), lambda p: (0, 0)),
            pl.BlockSpec((states, points), lambda p: (0, 0)),
            pl.BlockSpec((states, points), lambda p: (0, 0)),
            pl.BlockSpec((rows, 1), lambda p: (0, 0)),
            pl.BlockSpec((1, rows), lambda p: (0, 0)),
        ],
        out_specs=(
            pl.BlockSpec((lines, trio), lambda p: (0, p)),
            pl.BlockSpec((1, 4, wide, wide), lambda p: (p, 0, 0, 0)),
            pl.BlockSpec((2 * LANES, LANES), lambda p: (0, 0)),
            pl.BlockSpec((rows, OWNERS * rows), lambda p: (0, 0)),
            pl.BlockSpec((rim_rows, trio), lambda p: (0, 0)),
        ),
        scratch_shapes=[
            pltpu.VMEM((8, wide), F32),
            pltpu.VMEM((8, wide), F32),
            pltpu.VMEM((8, wide), F32),
            pltpu.VMEM((8, wide), F32),
            pltpu.VMEM((wide, 8), F32),
            pltpu.VMEM((wide, 8), F32),
            pltpu.VMEM((4 * rows, trio), F32),
            pltpu.VMEM((lines, trio), F32),
        ],
        compiler_params=pltpu.CompilerParams(vmem_limit_bytes=48 * 2**20),
        cost_estimate=pl.CostEstimate(flops=20_000_000, bytes_accessed=6_000_000, transcendentals=400_000),
        name="local",
    )(
        omega,
        phase,
        live,
        place,
        u,
        source,
        stencil.reshape(rows, 4 * points),
        line_coupling,
        line_diag,
        match_owner.reshape(rows, 1),
        match_row.reshape(1, rows),
    )

    whole = lambda array: pl.BlockSpec(array.shape, lambda p: (0, 0))
    edge = lambda array: pl.BlockSpec((array.shape[0], trio), lambda p: (0, p))
    updated = pl.pallas_call(
        functools.partial(finish_kernel, (times, cx, cz, pairs, points), len(far)),
        out_shape=jax.ShapeDtypeStruct((lines, width), F32),
        grid=(pairs,),
        in_specs=[smem]
        + [whole(piece) for piece in far]
        + [
            edge(work),
            pl.BlockSpec((1, 4, wide, wide), lambda p: (p, 0, 0, 0)),
            whole(shift),
            whole(pick),
            whole(rim_weights),
            edge(from_west),
            edge(from_east),
            edge(from_south),
            edge(from_north),
        ],
        out_specs=edge(work),
        scratch_shapes=[
            pltpu.VMEM((OWNERS * rows, LANES), BF16),
            pltpu.VMEM((rows, LANES), F32),
            pltpu.VMEM((cx * 8, trio), F32),
            pltpu.VMEM((cx * 8, trio), F32),
            pltpu.VMEM((2, lines, wide), BF16),
            pltpu.VMEM((2, lines, wide), BF16),
        ],
        compiler_params=pltpu.CompilerParams(vmem_limit_bytes=48 * 2**20),
        cost_estimate=pl.CostEstimate(flops=800_000_000, bytes_accessed=5_000_000, transcendentals=0),
        name="finish",
    )(live, *far, work, green, shift, pick, rim_weights, from_west, from_east, from_south, from_north)
    return updated.reshape(times, cx, cz, width)


def solution(mesh):
    in_specs = (
        P(None, "stream", "span", None),
        P(None, "stream", "span", None),
        P("stream", "span", None),
        P(),
        P(),
        P(),
        P(),
        P("stream", "span", None, None),
        P("stream", "span", None),
        P("stream", "span"),
    )
    out_specs = P(None, "stream", "span", None)
    return jax.shard_map(body, mesh=mesh, in_specs=in_specs, out_specs=out_specs, check_vma=False)
```

profile of v0, /device:TPU:449, one launch (start us, length us, event | category | flops | bytes accessed | tf_op | source)
XLA Modules:
  0.0 89.1 jit_solution(5032036972153360584)
XLA Ops:
  0.0 0.0 copy-start
  0.0 0.0 copy-start.6
  0.0 0.0 copy-start.5
  0.0 0.0 copy-start.4
  0.0 0.0 copy-start.3
  0.0 2.6 %edges.1 = (bf16[56,1152]{1,0:T(8,128)(2,1)}, bf16[56,1152]{1,0:T(8,128)(2,1)}, bf16[48,1152]{1,0:T(8,128)(2,1)}, bf16[48,1152]{1,0:T(8,128)(2,1)}, bf16[48,128]{1,0:T(8,128)(2,1)}) custom-call(f32[336,1152]{1,0:T(8,128)} %bitcast.9), custom_call_target="tpu_custom_call" | custom-call | tf_op jit(solution)/shard_map/edges/pallas_call | solution.py:366
  2.6 2.6 %collective-permute-start = (bf16[48,128]{1,0:T(8,128)(2,1)}, bf16[48,128]{1,0:T(8,128)(2,1)S(1)}, u32[]{:S(2)}, u32[]{:S(2)}) collective-permute-start(bf16[48,128]{1,0:T(8,128)(2,1)} %get-tuple-element.15), channel_id=1, source_target_pairs={{8,0},{16,8},{24,16},{32,24},{40,32},{48,40},{56,48},{64,56},{72,6... | collective-permute-start | bytes 36872 | tf_op jit(solution)/shard_map/ppermute | solution.py:384
  5.2 3.2 %collective-permute-start.7 = (bf16[48,1152]{1,0:T(8,128)(2,1)}, bf16[48,1152]{1,0:T(8,128)(2,1)S(1)}, u32[]{:S(2)}, u32[]{:S(2)}) collective-permute-start(bf16[48,1152]{1,0:T(8,128)(2,1)} %get-tuple-element.23), channel_id=1, source_target_pairs={{0,1},{1,2},{2,3},{3,4},{4,5},{5,6},{6,7},{8,9},{9,10},{10,11},{11... | collective-permute-start | bytes 331784 | tf_op jit(solution)/shard_map/ppermute | solution.py:391
  8.4 12.9 %collective-permute-start.8 = (bf16[48,1152]{1,0:T(8,128)(2,1)}, bf16[48,1152]{1,0:T(8,128)(2,1)S(1)}, u32[]{:S(2)}, u32[]{:S(2)}) collective-permute-start(bf16[48,1152]{1,0:T(8,128)(2,1)} %get-tuple-element.24), channel_id=1, source_target_pairs={{1,0},{2,1},{3,2},{4,3},{5,4},{6,5},{7,6},{9,8},{10,9},{11,10},{12... | collective-permute-start | bytes 331784 | tf_op jit(solution)/shard_map/ppermute | solution.py:392
  21.3 3.5 %collective-permute-start.5 = (bf16[56,1152]{1,0:T(8,128)(2,1)}, bf16[56,1152]{1,0:T(8,128)(2,1)S(1)}, u32[]{:S(2)}, u32[]{:S(2)}) collective-permute-start(bf16[56,1152]{1,0:T(8,128)(2,1)} %get-tuple-element.21), channel_id=1, source_target_pairs={{0,8},{8,16},{16,24},{24,32},{32,40},{40,48},{48,56},{56,64},{64,7... | collective-permute-start | bytes 387080 | tf_op jit(solution)/shard_map/ppermute | solution.py:389
  24.9 1.9 %collective-permute-start.6 = (bf16[56,1152]{1,0:T(8,128)(2,1)}, bf16[56,1152]{1,0:T(8,128)(2,1)S(1)}, u32[]{:S(2)}, u32[]{:S(2)}) collective-permute-start(bf16[56,1152]{1,0:T(8,128)(2,1)} %get-tuple-element.22), channel_id=1, source_target_pairs={{8,0},{16,8},{24,16},{32,24},{40,32},{48,40},{56,48},{64,56},{72,6... | collective-permute-start | bytes 387080 | tf_op jit(solution)/shard_map/ppermute | solution.py:390
  26.8 0.7 constant_dynamic-update-slice_fusion.1
  27.5 0.0 collective-permute-done
  27.5 6.1 %collective-permute-start.4 = (bf16[96,128]{1,0:T(8,128)(2,1)S(1)}, bf16[96,128]{1,0:T(8,128)(2,1)S(1)}, u32[]{:S(2)}, u32[]{:S(2)}) collective-permute-start(bf16[96,128]{1,0:T(8,128)(2,1)S(1)} %constant_dynamic-update-slice_fusion), channel_id=1, source_target_pairs={{280,0},{288,8},{296,16},{304,24},{312,32},{320,40},{328,48},{336,... | collective-permute-start | bytes 73736 | tf_op jit(solution)/shard_map/ppermute | solution.py:386
  33.6 15.2 %collective-permute-done.4.refs_3_ = bf16[96,128]{1,0:T(8,128)(2,1)S(1)} collective-permute-done((bf16[96,128]{1,0:T(8,128)(2,1)S(1)}, bf16[96,128]{1,0:T(8,128)(2,1)S(1)}, u32[]{:S(2)}, u32[]{:S(2)}) %collective-permute-start.4) | collective-permute-done | bytes 24608 | tf_op jit(solution)/shard_map/ppermute | solution.py:386
  48.8 1.9 %collective-permute-start.3 = (bf16[96,128]{1,0:T(8,128)(2,1)S(1)}, bf16[96,128]{1,0:T(8,128)(2,1)S(1)}, u32[]{:S(2)}, u32[]{:S(2)}) collective-permute-start(bf16[96,128]{1,0:T(8,128)(2,1)S(1)} %constant_dynamic-update-slice_fusion), channel_id=1, source_target_pairs={{264,0},{272,8},{280,16},{288,24},{296,32},{304,40},{312,48},{320,... | collective-permute-start | bytes 73736 | tf_op jit(solution)/shard_map/ppermute | solution.py:386
  50.7 5.6 %collective-permute-done.3.refs_2_ = bf16[96,128]{1,0:T(8,128)(2,1)S(1)} collective-permute-done((bf16[96,128]{1,0:T(8,128)(2,1)S(1)}, bf16[96,128]{1,0:T(8,128)(2,1)S(1)}, u32[]{:S(2)}, u32[]{:S(2)}) %collective-permute-start.3) | collective-permute-done | bytes 24608 | tf_op jit(solution)/shard_map/ppermute | solution.py:386
  56.3 1.9 %collective-permute-start.2 = (bf16[96,128]{1,0:T(8,128)(2,1)S(1)}, bf16[96,128]{1,0:T(8,128)(2,1)S(1)}, u32[]{:S(2)}, u32[]{:S(2)}) collective-permute-start(bf16[96,128]{1,0:T(8,128)(2,1)S(1)} %constant_dynamic-update-slice_fusion), channel_id=1, source_target_pairs={{248,0},{256,8},{264,16},{272,24},{280,32},{288,40},{296,48},{304,... | collective-permute-start | bytes 73736 | tf_op jit(solution)/shard_map/ppermute | solution.py:386
  58.3 4.7 %collective-permute-done.2.refs_1_ = bf16[96,128]{1,0:T(8,128)(2,1)S(1)} collective-permute-done((bf16[96,128]{1,0:T(8,128)(2,1)S(1)}, bf16[96,128]{1,0:T(8,128)(2,1)S(1)}, u32[]{:S(2)}, u32[]{:S(2)}) %collective-permute-start.2) | collective-permute-done | bytes 24608 | tf_op jit(solution)/shard_map/ppermute | solution.py:386
  63.0 14.5 %collective-permute-start.1 = (bf16[96,128]{1,0:T(8,128)(2,1)S(1)}, bf16[96,128]{1,0:T(8,128)(2,1)S(1)}, u32[]{:S(2)}, u32[]{:S(2)}) collective-permute-start(bf16[96,128]{1,0:T(8,128)(2,1)S(1)} %constant_dynamic-update-slice_fusion), channel_id=1, source_target_pairs={{232,0},{240,8},{248,16},{256,24},{264,32},{272,40},{280,48},{288,... | collective-permute-start | bytes 73736 | tf_op jit(solution)/shard_map/ppermute | solution.py:386
  79.4 0.0 copy-done.6
  79.4 0.1 copy.11.owner_ref
  79.5 0.0 copy-done
  79.5 0.0 copy-done.5
  79.5 0.0 copy-done.4
  79.5 0.0 copy-done.3
  79.5 0.0 copy-start.1
  79.6 1.1 %copy-done.1 = bf16[7,6,8,1152]{3,2,1,0:T(8,128)(2,1)S(1)} copy-done((bf16[7,6,8,1152]{3,2,1,0:T(8,128)(2,1)S(1)}, bf16[7,6,8,1152]{3,2,1,0:T(8,128)(2,1)}, u32[]{:S(2)}) %copy-start.1) | copy-done | bytes 774168
  80.7 0.0 copy-start.2
  80.7 0.9 %copy-done.2 = f32[6,8,768]{2,1,0:T(8,128)S(1)} copy-done((f32[6,8,768]{2,1,0:T(8,128)S(1)}, f32[6,8,768]{2,1,0:T(8,128)}, u32[]{:S(2)}) %copy-start.2) | copy-done | bytes 147480
  81.6 4.3 %local.1 = (f32[336,1152]{1,0:T(8,128)S(1)}, bf16[3,4,256,256]{3,2,1,0:T(8,128)(2,1)S(1)}, bf16[256,128]{1,0:T(8,128)(2,1)S(1)}, bf16[48,384]{1,0:T(8,128)(2,1)S(1)}, f32[112,384]{1,0:T(8,128)S(1)}) custom-call(f32[1]{0:T(128)S(6)} %copy.13.omega_ref, f32[1]{0:T(128)S(6)} %copy.14.phase_ref, s32[1]{0:T(128)} %bitcast.7.live_ref, s32[1]{0:T(128)} %bitcast.2.place_ref, ...), custom_call_target="tpu_custom_call" | custom-call | flops 20000000 | bytes 6000000 | tf_op jit(solution)/shard_map/local/pallas_call | solution.py:398
  85.9 0.0 collective-permute-done.1.refs_0_
  85.9 0.0 collective-permute-done.7.refs_11_
  85.9 0.0 collective-permute-done.8.refs_12_
  85.9 0.0 collective-permute-done.5.refs_9_
  85.9 0.0 collective-permute-done.6.refs_10_
  85.9 3.1 %finish.1 = f32[336,1152]{1,0:T(8,128)} custom-call(s32[1]{0:T(128)} %bitcast.8.live_ref, bf16[96,128]{1,0:T(8,128)(2,1)S(1)} %collective-permute-done.1.refs_0_, bf16[96,128]{1,0:T(8,128)(2,1)S(1)} %collective-permute-done.2.refs_1_, bf16[96,128]{1,0:T(8,128)(2,1)S(1)} %collective-permute-done.3.refs_2_, ...), custom_call_target="tpu_custom_call" | custom-call | flops 800000000 | bytes 5000000 | tf_op jit(solution)/shard_map/finish/pallas_call | solution.py:457
  (1 shorter events, 0.0 us)
Async XLA Ops:
  0.0 79.5 %copy-start = (f32[7,6,8,1152]{3,2,1,0:T(8,128)S(1)}, f32[7,6,8,1152]{3,2,1,0:T(8,128)}, u32[]{:S(2)}) copy-start(f32[7,6,8,1152]{3,2,1,0:T(8,128)} %param.10) | copy-start | bytes 4644868
  0.0 79.4 %copy-start.6 = (s32[1,1,48,1]{2,3,1,0:T(1,128)S(1)}, s32[1,1,48,1]{2,3,1,0:T(1,128)}, u32[]{:S(2)}) copy-start(s32[1,1,48,1]{2,3,1,0:T(1,128)} %param.17) | copy-start | bytes 580
  0.0 79.5 %copy-start.5 = (s32[1,1,48]{2,1,0:T(1,128)S(1)}, s32[1,1,48]{2,1,0:T(1,128)}, u32[]{:S(2)}) copy-start(s32[1,1,48]{2,1,0:T(1,128)} %param.18) | copy-start | bytes 580
  0.0 79.5 %copy-start.4 = (f32[6,192]{1,0:T(8,128)S(1)}, f32[6,192]{1,0:T(8,128)}, u32[]{:S(2)}) copy-start(f32[6,192]{1,0:T(8,128)} %diag_ref.1) | copy-start | bytes 13828
  0.0 79.5 %copy-start.3 = (f32[6,192]{1,0:T(8,128)S(1)}, f32[6,192]{1,0:T(8,128)}, u32[]{:S(2)}) copy-start(f32[6,192]{1,0:T(8,128)} %coupling_ref.1) | copy-start | bytes 13828
  2.6 24.9 %collective-permute-start = (bf16[48,128]{1,0:T(8,128)(2,1)}, bf16[48,128]{1,0:T(8,128)(2,1)S(1)}, u32[]{:S(2)}, u32[]{:S(2)}) collective-permute-start(bf16[48,128]{1,0:T(8,128)(2,1)} %get-tuple-element.15), channel_id=1, source_target_pairs={{8,0},{16,8},{24,16},{32,24},{40,32},{48,40},{56,48},{64,56},{72,6... | collective-permute-start | bytes 36872 | tf_op jit(solution)/shard_map/ppermute | solution.py:384
  5.2 80.7 %collective-permute-start.7 = (bf16[48,1152]{1,0:T(8,128)(2,1)}, bf16[48,1152]{1,0:T(8,128)(2,1)S(1)}, u32[]{:S(2)}, u32[]{:S(2)}) collective-permute-start(bf16[48,1152]{1,0:T(8,128)(2,1)} %get-tuple-element.23), channel_id=1, source_target_pairs={{0,1},{1,2},{2,3},{3,4},{4,5},{5,6},{6,7},{8,9},{9,10},{10,11},{11... | collective-permute-start | bytes 331784 | tf_op jit(solution)/shard_map/ppermute | solution.py:391
  8.4 77.5 %collective-permute-start.8 = (bf16[48,1152]{1,0:T(8,128)(2,1)}, bf16[48,1152]{1,0:T(8,128)(2,1)S(1)}, u32[]{:S(2)}, u32[]{:S(2)}) collective-permute-start(bf16[48,1152]{1,0:T(8,128)(2,1)} %get-tuple-element.24), channel_id=1, source_target_pairs={{1,0},{2,1},{3,2},{4,3},{5,4},{6,5},{7,6},{9,8},{10,9},{11,10},{12... | collective-permute-start | bytes 331784 | tf_op jit(solution)/shard_map/ppermute | solution.py:392
  21.3 64.6 %collective-permute-start.5 = (bf16[56,1152]{1,0:T(8,128)(2,1)}, bf16[56,1152]{1,0:T(8,128)(2,1)S(1)}, u32[]{:S(2)}, u32[]{:S(2)}) collective-permute-start(bf16[56,1152]{1,0:T(8,128)(2,1)} %get-tuple-element.21), channel_id=1, source_target_pairs={{0,8},{8,16},{16,24},{24,32},{32,40},{40,48},{48,56},{56,64},{64,7... | collective-permute-start | bytes 387080 | tf_op jit(solution)/shard_map/ppermute | solution.py:389
  24.9 61.0 %collective-permute-start.6 = (bf16[56,1152]{1,0:T(8,128)(2,1)}, bf16[56,1152]{1,0:T(8,128)(2,1)S(1)}, u32[]{:S(2)}, u32[]{:S(2)}) collective-permute-start(bf16[56,1152]{1,0:T(8,128)(2,1)} %get-tuple-element.22), channel_id=1, source_target_pairs={{8,0},{16,8},{24,16},{32,24},{40,32},{48,40},{56,48},{64,56},{72,6... | collective-permute-start | bytes 387080 | tf_op jit(solution)/shard_map/ppermute | solution.py:390
  27.5 21.3 %collective-permute-start.4 = (bf16[96,128]{1,0:T(8,128)(2,1)S(1)}, bf16[96,128]{1,0:T(8,128)(2,1)S(1)}, u32[]{:S(2)}, u32[]{:S(2)}) collective-permute-start(bf16[96,128]{1,0:T(8,128)(2,1)S(1)} %constant_dynamic-update-slice_fusion), channel_id=1, source_target_pairs={{280,0},{288,8},{296,16},{304,24},{312,32},{320,40},{328,48},{336,... | collective-permute-start | bytes 73736 | tf_op jit(solution)/shard_map/ppermute | solution.py:386
  48.8 7.5 %collective-permute-start.3 = (bf16[96,128]{1,0:T(8,128)(2,1)S(1)}, bf16[96,128]{1,0:T(8,128)(2,1)S(1)}, u32[]{:S(2)}, u32[]{:S(2)}) collective-permute-start(bf16[96,128]{1,0:T(8,128)(2,1)S(1)} %constant_dynamic-update-slice_fusion), channel_id=1, source_target_pairs={{264,0},{272,8},{280,16},{288,24},{296,32},{304,40},{312,48},{320,... | collective-permute-start | bytes 73736 | tf_op jit(solution)/shard_map/ppermute | solution.py:386
  56.3 6.6 %collective-permute-start.2 = (bf16[96,128]{1,0:T(8,128)(2,1)S(1)}, bf16[96,128]{1,0:T(8,128)(2,1)S(1)}, u32[]{:S(2)}, u32[]{:S(2)}) collective-permute-start(bf16[96,128]{1,0:T(8,128)(2,1)S(1)} %constant_dynamic-update-slice_fusion), channel_id=1, source_target_pairs={{248,0},{256,8},{264,16},{272,24},{280,32},{288,40},{296,48},{304,... | collective-permute-start | bytes 73736 | tf_op jit(solution)/shard_map/ppermute | solution.py:386
  63.0 22.9 %collective-permute-start.1 = (bf16[96,128]{1,0:T(8,128)(2,1)S(1)}, bf16[96,128]{1,0:T(8,128)(2,1)S(1)}, u32[]{:S(2)}, u32[]{:S(2)}) collective-permute-start(bf16[96,128]{1,0:T(8,128)(2,1)S(1)} %constant_dynamic-update-slice_fusion), channel_id=1, source_target_pairs={{232,0},{240,8},{248,16},{256,24},{264,32},{272,40},{280,48},{288,... | collective-permute-start | bytes 73736 | tf_op jit(solution)/shard_map/ppermute | solution.py:386
  79.5 1.1 %copy-start.1 = (bf16[7,6,8,1152]{3,2,1,0:T(8,128)(2,1)S(1)}, bf16[7,6,8,1152]{3,2,1,0:T(8,128)(2,1)}, u32[]{:S(2)}) copy-start(bf16[7,6,8,1152]{3,2,1,0:T(8,128)(2,1)} %source_ref.1) | copy-start | bytes 2322436
  80.7 0.9 %copy-start.2 = (f32[6,8,768]{2,1,0:T(8,128)S(1)}, f32[6,8,768]{2,1,0:T(8,128)}, u32[]{:S(2)}) copy-start(f32[6,8,768]{2,1,0:T(8,128)} %param.12) | copy-start | bytes 442372
where the time goes:
time: 89.5 us; the launch traced here: 89.1 us
  starting transfers between devices  48.5 us (54%)
  waiting for transfers between devices  25.5 us (28%)
  Pallas kernels  10 us (11%)
  local copies, waits for them, and re-layouts  2.86 us (3%)
  between operations  2.12 us (2%)
    ppermute x4, waiting for transfers between devices, body(): lax.ppermute(rim_two, 'stream', around(count, count // 2 + offset))  25.5 us
    ppermute x4, starting transfers between devices, body(): lax.ppermute(rim_two, 'stream', around(count, count // 2 + offset))  24.4 us
    ppermute x1, starting transfers between devices, body(): from_north = lax.ppermute(south, 'span', span_down)  12.9 us
    pallas_call x1, Pallas kernels, body(): pl.pallas_call(functools.partial(local_kernel, (times, cx, cz, pairs, poi...  4.29 us
    ppermute x1, starting transfers between devices, body(): from_west = lax.ppermute(east, 'stream', up)  3.54 us
    ppermute x1, starting transfers between devices, body(): from_south = lax.ppermute(north, 'span', span_up)  3.2 us
    pallas_call x1, Pallas kernels, body(): pl.pallas_call(functools.partial(finish_kernel, (times, cx, cz, pairs, po...  3.11 us
    unnamed x15, local copies, waits for them, and re-layouts  2.76 us
  transfers between devices with their start and end apart: 9, of which 3 were waited for; matrix products, arithmetic and copies ran while one was open for 1% of the time, Pallas kernels for 5%

commit v1 on v0

--- a/solution.py
+++ b/solution.py
@@ -14,6 +14,9 @@
 HALF = 64
 REACH = 3
 OWNERS = 8
+VMEM_GRANT = 60 * 2**20
+GROUPS = 3
+PARTS = 1
 
 
 def iota(shape, dim):
@@ -25,25 +28,13 @@
     return high, (value - high.astype(F32)).astype(BF16)
 
 
-def edge_kernel(dims, u_ref, west_ref, east_ref, south_ref, north_ref, rim_ref):
+def edge_kernel(dims, u_ref, first_x_ref, second_x_ref, first_z_ref, second_z_ref, rim_ref):
     times, cx, cz, pairs = dims
     rows = cx * cz
     width = u_ref.shape[1]
-    take = lambda t, x: u_ref[t * rows + x * cz : t * rows + x * cz + cz, :]
-    west_ref[...] = jnp.concatenate([take(t, 0) for t in range(times)], 0).astype(BF16)
-    east_ref[...] = jnp.concatenate([take(t, cx - 1) for t in range(times)], 0).astype(BF16)
-    sub = iota((8, width), 0)
-    for ref, z in ((south_ref, 0), (north_ref, cz - 1)):
-        tiles = []
-        for x in range(cx):
-            tile = jnp.zeros((8, width), F32)
-            for t in range(times):
-                at = t * rows + x * cz + z
-                tile = jnp.where(sub == t, u_ref[at : at + 1, :], tile)
-            tiles.append(tile)
-        ref[...] = jnp.concatenate(tiles, 0).astype(BF16)
     lane = iota((rows, LANES), 1)
     inner = lane % HALF
+    span = times * pairs
     found = jnp.zeros((rows, LANES), F32)
     for t in range(times):
         for pair in range(pairs):
@@ -55,13 +46,36 @@
             spot = t * pairs + pair
             both = pltpu.roll(both, (spot - (HALF - 1)) % LANES, 1)
             found = jnp.where(inner == spot, both, found)
-    high = found.astype(BF16).astype(F32)
-    rest = found - high
-    middle = rest.astype(BF16).astype(F32)
-    low = rest - middle
-    span = times * pairs
-    rim = high + pltpu.roll(middle, span, 1) + pltpu.roll(low, 2 * span, 1)
-    rim_ref[...] = rim.astype(BF16)
+    part = rows // GROUPS
+    parts = []
+    for _ in range(PARTS):
+        rounded = found.astype(BF16).astype(F32)
+        found = found - rounded
+        packed = rounded[:part]
+        for group in range(1, GROUPS):
+            packed = packed + pltpu.roll(rounded[group * part : (group + 1) * part], group * span, 1)
+        parts.append(packed)
+    packed = jnp.concatenate(parts, 0).astype(BF16)
+    for other in range(rim_ref.shape[0]):
+        rim_ref[other] = packed
+
+    take = lambda t, x: u_ref[t * rows + x * cz : t * rows + x * cz + cz, :]
+    west = jnp.concatenate([take(t, 0) for t in range(times)], 0)
+    east = jnp.concatenate([take(t, cx - 1) for t in range(times)], 0)
+    even_x = lax.axis_index("stream") % 2 == 0
+    first_x_ref[...] = jnp.where(even_x, east, west).astype(BF16)
+    second_x_ref[...] = jnp.where(even_x, west, east).astype(BF16)
+    sub = iota((8, width), 0)
+    even_z = lax.axis_index("span") % 2 == 0
+    top = cz - 1
+    for ref, z in ((first_z_ref, jnp.where(even_z, top, 0)), (second_z_ref, jnp.where(even_z, 0, top))):
+        tiles = []
+        for x in range(cx):
+            tile = jnp.zeros((8, width), F32)
+            for t in range(times):
+                tile = jnp.where(sub == t, u_ref[pl.ds(t * rows + x * cz + z, 1), :], tile)
+            tiles.append(tile)
+        ref[...] = jnp.concatenate(tiles, 0).astype(BF16)
 
 
 def scan_products(matrix, lane, points, backward):
@@ -86,7 +100,6 @@
     omega_ref,
     phase_ref,
     live_ref,
-    place_ref,
     u_ref,
     source_ref,
     stencil_ref,
@@ -98,6 +111,7 @@
     green_ref,
     shift_ref,
     pick_ref,
+    keep_ref,
     rimw_ref,
     couple_s,
     diag_s,
@@ -177,15 +191,20 @@
                 face = jnp.where(z == cz - 1, 0.0, face)
             face_s[way * rows : (way + 1) * rows, :] = face
 
-        slot = owner_ref[...] - place_ref[0] + (count // 2 + REACH)
+        slot = owner_ref[...] - lax.axis_index("stream") + (count // 2 + REACH)
         slot = jnp.where(slot < 0, slot + count, slot)
         slot = jnp.where(slot >= count, slot - count, slot)
         diagonal = iota((rows, rows), 0) == iota((rows, rows), 1)
         target = jnp.sum(jnp.where(diagonal, row_ref[...].astype(F32), 0.0), axis=1, keepdims=True)
         target = target.astype(jnp.int32)
-        wanted = slot * rows + target
-        cell = iota((rows, OWNERS * rows), 1)
+        part = rows // GROUPS
+        group = jnp.zeros_like(target)
+        for k in range(1, GROUPS):
+            group = group + jnp.where(target >= k * part, 1, 0)
+        wanted = slot * part + target - group * part
+        cell = iota((rows, OWNERS * part), 1)
         pick_ref[...] = jnp.where(cell == wanted, 1.0, 0.0).astype(BF16)
+        keep_ref[...] = jnp.where(iota((rows, LANES), 1) % HALF // span == group, 1.0, 0.0)
 
         left = iota((LANES, LANES), 0)
         right = iota((LANES, LANES), 1)
@@ -255,44 +274,55 @@
             work_ref[at(t, x), :] = jnp.where(z + x * cz < live, value, u_ref[at(t, x), :])
 
 
-def finish_kernel(dims, groups, live_ref, *refs):
-    times, cx, cz, pairs, points = dims
-    rim_refs = refs[:groups]
-    (
-        work_ref,
-        green_ref,
-        shift_ref,
-        pick_ref,
-        rimw_ref,
-        west_ref,
-        east_ref,
-        south_ref,
-        north_ref,
-        out_ref,
-        rim_s,
-        ghost_s,
-        south_s,
-        north_s,
-        high_s,
-        low_s,
-    ) = refs[groups:]
+def finish_kernel(
+    dims,
+    live_ref,
+    rim_ref,
+    work_ref,
+    green_ref,
+    shift_ref,
+    pick_ref,
+    keep_ref,
+    rimw_ref,
+    first_x_ref,
+    second_x_ref,
+    first_z_ref,
+    second_z_ref,
+    out_ref,
+    rim_s,
+    ghost_s,
+    south_s,
+    north_s,
+    high_s,
+    low_s,
+):
+    times, cx, cz, pairs, points, count = dims
     rows = cx * cz
+    part = rows // GROUPS
 
     @pl.when(pl.program_id(0) == 0)
     def ghosts():
-        at = 0
-        for ref in rim_refs:
-            rim_s[at : at + ref.shape[0], :] = ref[...]
-            at += ref.shape[0]
-        picked = jnp.dot(pick_ref[...], rim_s[...], preferred_element_type=F32).astype(BF16)
-        ghost = jnp.dot(picked, shift_ref[0:LANES, :], preferred_element_type=F32)
-        ghost += jnp.dot(picked, shift_ref[LANES : 2 * LANES, :], preferred_element_type=F32)
+        ghost = jnp.zeros((rows, LANES), F32)
+        for piece in range(PARTS):
+            for k in range(OWNERS):
+                owner = lax.rem(lax.axis_index("stream") + (count + count // 2 - REACH + k), count)
+                rim_s[k * part : (k + 1) * part, :] = rim_ref[owner, piece * part : (piece + 1) * part]
+            picked = jnp.dot(pick_ref[...], rim_s[...], preferred_element_type=F32)
+            picked = (picked * keep_ref[...]).astype(BF16)
+            ghost += jnp.dot(picked, shift_ref[0:LANES, :], preferred_element_type=F32)
+            ghost += jnp.dot(picked, shift_ref[LANES : 2 * LANES, :], preferred_element_type=F32)
         ghost_s[...] = ghost
 
-    west = west_ref[...].astype(F32)
-    east = east_ref[...].astype(F32)
-    south_s[...] = south_ref[...].astype(F32)
-    north_s[...] = north_ref[...].astype(F32)
+    first = first_x_ref[...].astype(F32)
+    second = second_x_ref[...].astype(F32)
+    even_x = lax.axis_index("stream") % 2 == 0
+    west = jnp.where(even_x, second, first)
+    east = jnp.where(even_x, first, second)
+    first = first_z_ref[...].astype(F32)
+    second = second_z_ref[...].astype(F32)
+    even_z = lax.axis_index("span") % 2 == 0
+    south_s[...] = jnp.where(even_z, second, first)
+    north_s[...] = jnp.where(even_z, first, second)
     lane = iota((cz, LANES), 1)
     inner = lane % HALF
     low_half = lane < HALF
@@ -336,8 +366,9 @@
         out_ref[:, lanes] = jnp.where(alive, tile, work_ref[:, lanes])
 
 
-def around(count, offset):
-    return [((i + offset) % count, i) for i in range(count)]
+def pairing(count, first):
+    up = [(i, i + 1) for i in range(first, count - 1, 2)]
+    return up + [(b, a) for a, b in up]
 
 
 def body(
@@ -363,50 +394,44 @@
     u = adjoint.reshape(lines, width)
     vmem = pl.BlockSpec(memory_space=pltpu.VMEM)
     smem = pl.BlockSpec(memory_space=pltpu.SMEM)
-    west, east, south, north, rim = pl.pallas_call(
+    part = rows // GROUPS
+    first_x, second_x, first_z, second_z, rim = pl.pallas_call(
         functools.partial(edge_kernel, (times, cx, cz, pairs)),
         out_shape=(
             jax.ShapeDtypeStruct((times * cz, width), BF16),
             jax.ShapeDtypeStruct((times * cz, width), BF16),
             jax.ShapeDtypeStruct((cx * 8, width), BF16),
             jax.ShapeDtypeStruct((cx * 8, width), BF16),
-            jax.ShapeDtypeStruct((rows, LANES), BF16),
+            jax.ShapeDtypeStruct((count, PARTS * part, LANES), BF16),
         ),
         in_specs=[vmem],
         out_specs=(vmem,) * 5,
+        compiler_params=pltpu.CompilerParams(vmem_limit_bytes=VMEM_GRANT),
         name="edges",
     )(u)
 
-    up = [(i, i + 1) for i in range(count - 1)]
-    down = [(i + 1, i) for i in range(count - 1)]
-    span_up = [(i, i + 1) for i in range(spans - 1)]
-    span_down = [(i + 1, i) for i in range(spans - 1)]
-    rim_two = jnp.concatenate([rim, lax.ppermute(rim, "stream", around(count, 1))], 0)
-    far = [
-        lax.ppermute(rim_two, "stream", around(count, count // 2 + offset))
-        for offset in range(-REACH, OWNERS - REACH, 2)
-    ]
-    from_west = lax.ppermute(east, "stream", up)
-    from_east = lax.ppermute(west, "stream", down)
-    from_south = lax.ppermute(north, "span", span_up)
-    from_north = lax.ppermute(south, "span", span_down)
+    rims = lax.all_to_all(rim, "stream", 0, 0)
+    first_x = lax.ppermute(first_x, "stream", pairing(count, 0))
+    second_z, second_x, _ = lax.optimization_barrier((second_z, second_x, first_x))
+    second_z = lax.ppermute(second_z, "span", pairing(spans, 1))
+    second_x = lax.ppermute(second_x, "stream", pairing(count, 1))
+    first_z = lax.ppermute(first_z, "span", pairing(spans, 0))
 
     live = tile_live.reshape(1)
-    place = lax.axis_index("stream").astype(jnp.int32).reshape(1)
     trio = 3 * LANES
     rim_rows = 2 * cz + 2 * rows
-    work, green, shift, pick, rim_weights = pl.pallas_call(
+    work, green, shift, pick, keep, rim_weights = pl.pallas_call(
         functools.partial(local_kernel, (times, cx, cz, pairs, points, count)),
         out_shape=(
             jax.ShapeDtypeStruct((lines, width), F32),
             jax.ShapeDtypeStruct((pairs, 4, wide, wide), BF16),
             jax.ShapeDtypeStruct((2 * LANES, LANES), BF16),
-            jax.ShapeDtypeStruct((rows, OWNERS * rows), BF16),
+            jax.ShapeDtypeStruct((rows, OWNERS * part), BF16),
+            jax.ShapeDtypeStruct((rows, LANES), F32),
             jax.ShapeDtypeStruct((rim_rows, trio), F32),
         ),
         grid=(pairs,),
         in_specs=[
-            smem,
             smem,
             smem,
             smem,
@@ -422,7 +447,8 @@
             pl.BlockSpec((lines, trio), lambda p: (0, p)),
             pl.BlockSpec((1, 4, wide, wide), lambda p: (p, 0, 0, 0)),
             pl.BlockSpec((2 * LANES, LANES), lambda p: (0, 0)),
-            pl.BlockSpec((rows, OWNERS * rows), lambda p: (0, 0)),
+            pl.BlockSpec((rows, OWNERS * part), lambda p: (0, 0)),
+            pl.BlockSpec((rows, LANES), lambda p: (0, 0)),
             pl.BlockSpec((rim_rows, trio), lambda p: (0, 0)),
         ),
         scratch_shapes=[
@@ -435,14 +461,13 @@
             pltpu.VMEM((4 * rows, trio), F32),
             pltpu.VMEM((lines, trio), F32),
         ],
-        compiler_params=pltpu.CompilerParams(vmem_limit_bytes=48 * 2**20),
+        compiler_params=pltpu.CompilerParams(vmem_limit_bytes=VMEM_GRANT),
         cost_estimate=pl.CostEstimate(flops=20_000_000, bytes_accessed=6_000_000, transcendentals=400_000),
         name="local",
     )(
         omega,
         phase,
         live,
-        place,
         u,
         source,
         stencil.reshape(rows, 4 * points),
@@ -455,35 +480,49 @@
     whole = lambda array: pl.BlockSpec(array.shape, lambda p: (0, 0))
     edge = lambda array: pl.BlockSpec((array.shape[0], trio), lambda p: (0, p))
     updated = pl.pallas_call(
-        functools.partial(finish_kernel, (times, cx, cz, pairs, points), len(far)),
+        functools.partial(finish_kernel, (times, cx, cz, pairs, points, count)),
         out_shape=jax.ShapeDtypeStruct((lines, width), F32),
         grid=(pairs,),
-        in_specs=[smem]
-        + [whole(piece) for piece in far]
-        + [
+        in_specs=[
+            smem,
+            pl.BlockSpec(rims.shape, lambda p: (0, 0, 0)),
             edge(work),
             pl.BlockSpec((1, 4, wide, wide), lambda p: (p, 0, 0, 0)),
             whole(shift),
             whole(pick),
+            whole(keep),
             whole(rim_weights),
-            edge(from_west),
-            edge(from_east),
-            edge(from_south),
-            edge(from_north),
+            edge(first_x),
+            edge(second_x),
+            edge(first_z),
+            edge(second_z),
         ],
         out_specs=edge(work),
         scratch_shapes=[
-            pltpu.VMEM((OWNERS * rows, LANES), BF16),
+            pltpu.VMEM((OWNERS * part, LANES), BF16),
             pltpu.VMEM((rows, LANES), F32),
             pltpu.VMEM((cx * 8, trio), F32),
             pltpu.VMEM((cx * 8, trio), F32),
             pltpu.VMEM((2, lines, wide), BF16),
             pltpu.VMEM((2, lines, wide), BF16),
         ],
-        compiler_params=pltpu.CompilerParams(vmem_limit_bytes=48 * 2**20),
+        compiler_params=pltpu.CompilerParams(vmem_limit_bytes=VMEM_GRANT),
         cost_estimate=pl.CostEstimate(flops=800_000_000, bytes_accessed=5_000_000, transcendentals=0),
         name="finish",
-    )(live, *far, work, green, shift, pick, rim_weights, from_west, from_east, from_south, from_north)
+    )(
+        live,
+        rims,
+        work,
+        green,
+        shift,
+        pick,
+        keep,
+        rim_weights,
+        first_x,
+        second_x,
+        first_z,
+        second_z,
+    )
     return updated.reshape(times, cx, cz, width)
 
 

time: 89.5 us -> 59.6 us (0.67)
  the two profiles are of different devices: /device:TPU:449 before, /device:TPU:30 now
where the time goes in v1:
time: 59.6 us; the launch traced here: 59.2 us
  starting transfers between devices  39.6 us (66%)
  Pallas kernels  14.7 us (25%)
  between operations  2.06 us (3%)
  local copies, waits for them, and re-layouts  1.44 us (2%)
  waiting for transfers between devices  1.39 us (2%)
    all_to_all x1, starting transfers between devices, body(): rims = lax.all_to_all(rim, 'stream', 0, 0)  16.2 us
    ppermute x1, starting transfers between devices, body(): second_x = lax.ppermute(second_x, 'stream', pairing(count, 1))  10 us
    ppermute x1, starting transfers between devices, body(): second_z = lax.ppermute(second_z, 'span', pairing(spans, 1))  8.71 us
    pallas_call x1, Pallas kernels, body(): pl.pallas_call(functools.partial(local_kernel, (times, cx, cz, pairs, poi...  7.02 us
    pallas_call x1, Pallas kernels, body(): pl.pallas_call(functools.partial(finish_kernel, (times, cx, cz, pairs, po...  5.1 us
    ppermute x1, starting transfers between devices, body(): first_z = lax.ppermute(first_z, 'span', pairing(spans, 0))  2.65 us
    pallas_call x1, Pallas kernels, body(): pl.pallas_call(functools.partial(edge_kernel, (times, cx, cz, pairs)), ou...  2.56 us
    ppermute x1, starting transfers between devices, body(): first_x = lax.ppermute(first_x, 'stream', pairing(count, 0))  2.06 us
  transfers between devices with their start and end apart: 5, of which 1 were waited for; matrix products, arithmetic and copies ran while one was open for 1% of the time, Pallas kernels for 12%

profile of v1, /device:TPU:30, one launch (start us, length us, event | category | flops | bytes accessed | tf_op | source)
XLA Modules:
  0.0 59.2 jit_solution(7049600327283961881)
XLA Ops:
  0.0 0.0 copy-start.5
  0.0 2.6 %edges.1 = (bf16[56,1152]{1,0:T(8,128)(2,1)}, bf16[56,1152]{1,0:T(8,128)(2,1)}, bf16[48,1152]{1,0:T(8,128)(2,1)}, bf16[48,1152]{1,0:T(8,128)(2,1)}, bf16[64,16,128]{2,1,0:T(8,128)(2,1)}) custom-call(f32[336,1152]{1,0:T(8,128)} %bitcast.8), custom_call_target="tpu_custom_call" | custom-call | tf_op jit(solution)/shard_map/edges/pallas_call | solution.py:398
  2.6 16.2 %all-to-all-start = ((bf16[64,16,128]{2,1,0:T(8,128)(2,1)}), bf16[64,16,128]{2,1,0:T(8,128)(2,1)S(1)}, u32[]{:S(2)}, u32[]{:S(2)}) async-start(bf16[64,16,128]{2,1,0:T(8,128)(2,1)} %get-tuple-element.18), calls=%async_computation | async-start | bytes 524288 | tf_op jit(solution)/shard_map/all_to_all | solution.py:413
  18.8 2.1 %collective-permute-start = (bf16[56,1152]{1,0:T(8,128)(2,1)}, bf16[56,1152]{1,0:T(8,128)(2,1)S(1)}, u32[]{:S(2)}, u32[]{:S(2)}) collective-permute-start(bf16[56,1152]{1,0:T(8,128)(2,1)} %get-tuple-element.25), channel_id=1, source_target_pairs={{0,8},{16,24},{32,40},{48,56},{64,72},{80,88},{96,104},{112,120},{... | collective-permute-start | bytes 387080 | tf_op jit(solution)/shard_map/ppermute | solution.py:414
  20.9 1.4 %collective-permute-done.first_x_ref = bf16[56,1152]{1,0:T(8,128)(2,1)S(1)} collective-permute-done((bf16[56,1152]{1,0:T(8,128)(2,1)}, bf16[56,1152]{1,0:T(8,128)(2,1)S(1)}, u32[]{:S(2)}, u32[]{:S(2)}) %collective-permute-start) | collective-permute-done | bytes 129056 | tf_op jit(solution)/shard_map/ppermute | solution.py:414
  22.2 0.0 copy-start.1
  22.2 10.0 %collective-permute-start.1 = (bf16[56,1152]{1,0:T(8,128)(2,1)}, bf16[56,1152]{1,0:T(8,128)(2,1)S(1)}, u32[]{:S(2)}, u32[]{:S(2)}) collective-permute-start(bf16[56,1152]{1,0:T(8,128)(2,1)} %get-tuple-element.28), channel_id=1, source_target_pairs={{8,16},{24,32},{40,48},{56,64},{72,80},{88,96},{104,112},{120,128}... | collective-permute-start | bytes 387080 | tf_op jit(solution)/shard_map/ppermute | solution.py:417
  32.3 2.7 %collective-permute-start.2 = (bf16[48,1152]{1,0:T(8,128)(2,1)}, bf16[48,1152]{1,0:T(8,128)(2,1)S(1)}, u32[]{:S(2)}, u32[]{:S(2)}) collective-permute-start(bf16[48,1152]{1,0:T(8,128)(2,1)} %get-tuple-element.29), channel_id=1, source_target_pairs={{0,1},{2,3},{4,5},{6,7},{1,0},{3,2},{5,4},{7,6},{8,9},{10,11},{12,... | collective-permute-start | bytes 331784 | tf_op jit(solution)/shard_map/ppermute | solution.py:418
  34.9 8.7 %collective-permute-start.3 = (bf16[48,1152]{1,0:T(8,128)(2,1)}, bf16[48,1152]{1,0:T(8,128)(2,1)S(1)}, u32[]{:S(2)}, u32[]{:S(2)}) collective-permute-start(bf16[48,1152]{1,0:T(8,128)(2,1)} %get-tuple-element.30), channel_id=1, source_target_pairs={{1,2},{3,4},{5,6},{2,1},{4,3},{6,5},{9,10},{11,12},{13,14},{10,9},... | collective-permute-start | bytes 331784 | tf_op jit(solution)/shard_map/ppermute | solution.py:416
  45.6 0.0 copy-done.5
  45.6 0.7 %copy.11.owner_ref = s32[48,1]{1,0:T(8,128)} copy(s32[48,1]{0,1:T(1,128)S(1)} %bitcast.11) | data formatting | bytes 384 | tf_op jit(solution)/shard_map/reshape | solution.py:476
  46.3 7.0 %local.1 = (f32[336,1152]{1,0:T(8,128)}, bf16[3,4,256,256]{3,2,1,0:T(8,128)(2,1)}, bf16[256,128]{1,0:T(8,128)(2,1)}, bf16[48,128]{1,0:T(8,128)(2,1)}, f32[48,128]{1,0:T(8,128)}, /*index=5*/f32[112,384]{1,0:T(8,128)}) custom-call(f32[1]{0:T(128)S(6)} %copy.12.omega_ref, f32[1]{0:T(128)S(6)} %copy.13.phase_ref, s32[1]{0:T(128)} %bitcast.6.live_ref, ...), custom_call_target="tpu_custom_call" | custom-call | flops 20000000 | bytes 6000000 | tf_op jit(solution)/shard_map/local/pallas_call | solution.py:423
  53.3 0.0 collective-permute-done.2.first_z_ref
  53.3 0.0 copy-start.3
  53.3 0.0 collective-permute-done.3.second_z_ref
  53.3 0.0 copy-start.4
  53.3 0.0 collective-permute-done.1.second_x_ref
  53.3 0.0 copy-start.2
  53.4 0.0 all-to-all-done.rim_ref
  53.4 0.0 copy-start
  53.4 0.0 copy-done.1
  53.4 0.6 copy-done.3
  54.0 0.0 copy-done.4
  54.0 0.0 copy-done.2
  54.0 0.1 copy-done
  54.1 5.1 %finish.1 = f32[336,1152]{1,0:T(8,128)} custom-call(s32[1]{0:T(128)} %bitcast.7.live_ref, bf16[64,16,128]{2,1,0:T(8,128)(2,1)} %copy-done, f32[336,1152]{1,0:T(8,128)} %get-tuple-element.19.work_ref, bf16[3,4,256,256]{3,2,1,0:T(8,128)(2,1)} %get-tuple-element.20.green_ref, bf16[256,128]{1,0:T(8,128)(2,1)} %get-tuple-element.21.shift_ref, ...), custom_call_target="tpu_custom_call" | custom-call | flops 800000000 | bytes 5000000 | tf_op jit(solution)/shard_map/finish/pallas_call | solution.py:482
Async XLA Ops:
  0.0 45.6 %copy-start.5 = (s32[1,1,48,1]{2,3,1,0:T(1,128)S(1)}, s32[1,1,48,1]{2,3,1,0:T(1,128)}, u32[]{:S(2)}) copy-start(s32[1,1,48,1]{2,3,1,0:T(1,128)} %param.17) | copy-start | bytes 580
  2.6 50.8 %all-to-all-start = ((bf16[64,16,128]{2,1,0:T(8,128)(2,1)}), bf16[64,16,128]{2,1,0:T(8,128)(2,1)S(1)}, u32[]{:S(2)}, u32[]{:S(2)}) async-start(bf16[64,16,128]{2,1,0:T(8,128)(2,1)} %get-tuple-element.18), calls=%async_computation | async-start | bytes 524288 | tf_op jit(solution)/shard_map/all_to_all | solution.py:413
  18.8 3.4 %collective-permute-start = (bf16[56,1152]{1,0:T(8,128)(2,1)}, bf16[56,1152]{1,0:T(8,128)(2,1)S(1)}, u32[]{:S(2)}, u32[]{:S(2)}) collective-permute-start(bf16[56,1152]{1,0:T(8,128)(2,1)} %get-tuple-element.25), channel_id=1, source_target_pairs={{0,8},{16,24},{32,40},{48,56},{64,72},{80,88},{96,104},{112,120},{... | collective-permute-start | bytes 387080 | tf_op jit(solution)/shard_map/ppermute | solution.py:414
  22.2 31.1 %copy-start.1 = (bf16[56,1152]{1,0:T(8,128)(2,1)}, bf16[56,1152]{1,0:T(8,128)(2,1)S(1)}, u32[]{:S(2)}) copy-start(bf16[56,1152]{1,0:T(8,128)(2,1)S(1)} %collective-permute-done.first_x_ref) | copy-start | bytes 387076
  22.2 31.1 %collective-permute-start.1 = (bf16[56,1152]{1,0:T(8,128)(2,1)}, bf16[56,1152]{1,0:T(8,128)(2,1)S(1)}, u32[]{:S(2)}, u32[]{:S(2)}) collective-permute-start(bf16[56,1152]{1,0:T(8,128)(2,1)} %get-tuple-element.28), channel_id=1, source_target_pairs={{8,16},{24,32},{40,48},{56,64},{72,80},{88,96},{104,112},{120,128}... | collective-permute-start | bytes 387080 | tf_op jit(solution)/shard_map/ppermute | solution.py:417
  32.3 21.1 %collective-permute-start.2 = (bf16[48,1152]{1,0:T(8,128)(2,1)}, bf16[48,1152]{1,0:T(8,128)(2,1)S(1)}, u32[]{:S(2)}, u32[]{:S(2)}) collective-permute-start(bf16[48,1152]{1,0:T(8,128)(2,1)} %get-tuple-element.29), channel_id=1, source_target_pairs={{0,1},{2,3},{4,5},{6,7},{1,0},{3,2},{5,4},{7,6},{8,9},{10,11},{12,... | collective-permute-start | bytes 331784 | tf_op jit(solution)/shard_map/ppermute | solution.py:418
  34.9 18.4 %collective-permute-start.3 = (bf16[48,1152]{1,0:T(8,128)(2,1)}, bf16[48,1152]{1,0:T(8,128)(2,1)S(1)}, u32[]{:S(2)}, u32[]{:S(2)}) collective-permute-start(bf16[48,1152]{1,0:T(8,128)(2,1)} %get-tuple-element.30), channel_id=1, source_target_pairs={{1,2},{3,4},{5,6},{2,1},{4,3},{6,5},{9,10},{11,12},{13,14},{10,9},... | collective-permute-start | bytes 331784 | tf_op jit(solution)/shard_map/ppermute | solution.py:416
  53.3 0.7 %copy-start.3 = (bf16[48,1152]{1,0:T(8,128)(2,1)}, bf16[48,1152]{1,0:T(8,128)(2,1)S(1)}, u32[]{:S(2)}) copy-start(bf16[48,1152]{1,0:T(8,128)(2,1)S(1)} %collective-permute-done.2.first_z_ref) | copy-start | bytes 331780
  53.3 0.7 %copy-start.4 = (bf16[48,1152]{1,0:T(8,128)(2,1)}, bf16[48,1152]{1,0:T(8,128)(2,1)S(1)}, u32[]{:S(2)}) copy-start(bf16[48,1152]{1,0:T(8,128)(2,1)S(1)} %collective-permute-done.3.second_z_ref) | copy-start | bytes 331780
  53.3 0.7 %copy-start.2 = (bf16[56,1152]{1,0:T(8,128)(2,1)}, bf16[56,1152]{1,0:T(8,128)(2,1)S(1)}, u32[]{:S(2)}) copy-start(bf16[56,1152]{1,0:T(8,128)(2,1)S(1)} %collective-permute-done.1.second_x_ref) | copy-start | bytes 387076
  53.4 0.8 %copy-start = (bf16[64,16,128]{2,1,0:T(8,128)(2,1)}, bf16[64,16,128]{2,1,0:T(8,128)(2,1)S(1)}, u32[]{:S(2)}) copy-start(bf16[64,16,128]{2,1,0:T(8,128)(2,1)S(1)} %all-to-all-done.rim_ref) | copy-start | bytes 786436

commit v2 on v1

--- a/solution.py
+++ b/solution.py
@@ -28,7 +28,7 @@
     return high, (value - high.astype(F32)).astype(BF16)
 
 
-def edge_kernel(dims, u_ref, first_x_ref, second_x_ref, first_z_ref, second_z_ref, rim_ref):
+def edge_kernel(dims, u_ref, rim_ref, second_z_ref, second_x_ref, first_z_ref, first_x_ref):
     times, cx, cz, pairs = dims
     rows = cx * cz
     width = u_ref.shape[1]
@@ -284,10 +284,10 @@
     pick_ref,
     keep_ref,
     rimw_ref,
-    first_x_ref,
+    second_z_ref,
     second_x_ref,
     first_z_ref,
-    second_z_ref,
+    first_x_ref,
     out_ref,
     rim_s,
     ghost_s,
@@ -395,14 +395,14 @@
     vmem = pl.BlockSpec(memory_space=pltpu.VMEM)
     smem = pl.BlockSpec(memory_space=pltpu.SMEM)
     part = rows // GROUPS
-    first_x, second_x, first_z, second_z, rim = pl.pallas_call(
+    rim, second_z, second_x, first_z, first_x = pl.pallas_call(
         functools.partial(edge_kernel, (times, cx, cz, pairs)),
         out_shape=(
-            jax.ShapeDtypeStruct((times * cz, width), BF16),
+            jax.ShapeDtypeStruct((count, PARTS * part, LANES), BF16),
+            jax.ShapeDtypeStruct((cx * 8, width), BF16),
             jax.ShapeDtypeStruct((times * cz, width), BF16),
             jax.ShapeDtypeStruct((cx * 8, width), BF16),
-            jax.ShapeDtypeStruct((cx * 8, width), BF16),
-            jax.ShapeDtypeStruct((count, PARTS * part, LANES), BF16),
+            jax.ShapeDtypeStruct((times * cz, width), BF16),
         ),
         in_specs=[vmem],
         out_specs=(vmem,) * 5,
@@ -411,10 +411,9 @@
     )(u)
 
     rims = lax.all_to_all(rim, "stream", 0, 0)
-    first_x = lax.ppermute(first_x, "stream", pairing(count, 0))
-    second_z, second_x, _ = lax.optimization_barrier((second_z, second_x, first_x))
     second_z = lax.ppermute(second_z, "span", pairing(spans, 1))
     second_x = lax.ppermute(second_x, "stream", pairing(count, 1))
+    first_x = lax.ppermute(first_x, "stream", pairing(count, 0))
     first_z = lax.ppermute(first_z, "span", pairing(spans, 0))
 
     live = tile_live.reshape(1)
@@ -423,12 +422,12 @@
     work, green, shift, pick, keep, rim_weights = pl.pallas_call(
         functools.partial(local_kernel, (times, cx, cz, pairs, points, count)),
         out_shape=(
-            jax.ShapeDtypeStruct((lines, width), F32),
-            jax.ShapeDtypeStruct((pairs, 4, wide, wide), BF16),
-            jax.ShapeDtypeStruct((2 * LANES, LANES), BF16),
-            jax.ShapeDtypeStruct((rows, OWNERS * part), BF16),
-            jax.ShapeDtypeStruct((rows, LANES), F32),
-            jax.ShapeDtypeStruct((rim_rows, trio), F32),
+            pltpu.HBM((lines, width), F32),
+            pltpu.HBM((pairs, 4, wide, wide), BF16),
+            pltpu.HBM((2 * LANES, LANES), BF16),
+            pltpu.HBM((rows, OWNERS * part), BF16),
+            pltpu.HBM((rows, LANES), F32),
+            pltpu.HBM((rim_rows, trio), F32),
         ),
         grid=(pairs,),
         in_specs=[
@@ -461,7 +460,7 @@
             pltpu.VMEM((4 * rows, trio), F32),
             pltpu.VMEM((lines, trio), F32),
         ],
-        compiler_params=pltpu.CompilerParams(vmem_limit_bytes=VMEM_GRANT),
+        compiler_params=pltpu.CompilerParams(vmem_limit_bytes=16 * 2**20),
         cost_estimate=pl.CostEstimate(flops=20_000_000, bytes_accessed=6_000_000, transcendentals=400_000),
         name="local",
     )(
@@ -492,10 +491,10 @@
             whole(pick),
             whole(keep),
             whole(rim_weights),
-            edge(first_x),
+            edge(second_z),
             edge(second_x),
             edge(first_z),
-            edge(second_z),
+            edge(first_x),
         ],
         out_specs=edge(work),
         scratch_shapes=[
@@ -506,7 +505,7 @@
             pltpu.VMEM((2, lines, wide), BF16),
             pltpu.VMEM((2, lines, wide), BF16),
         ],
-        compiler_params=pltpu.CompilerParams(vmem_limit_bytes=VMEM_GRANT),
+        compiler_params=pltpu.CompilerParams(vmem_limit_bytes=65400 * 2**10),
         cost_estimate=pl.CostEstimate(flops=800_000_000, bytes_accessed=5_000_000, transcendentals=0),
         name="finish",
     )(
@@ -518,10 +517,10 @@
         pick,
         keep,
         rim_weights,
-        first_x,
+        second_z,
         second_x,
         first_z,
-        second_z,
+        first_x,
     )
     return updated.reshape(times, cx, cz, width)
 

time: 59.6 us -> 56.4 us (0.946)
  the two profiles are of different devices: /device:TPU:30 before, /device:TPU:23 now
where the time goes in v2:
time: 56.4 us; the launch traced here: 56 us
  starting transfers between devices  39.5 us (70%)
  Pallas kernels  13.2 us (23%)
  between operations  2.08 us (4%)
  local copies, waits for them, and re-layouts  1.24 us (2%)
    all_to_all x1, starting transfers between devices, body(): rims = lax.all_to_all(rim, 'stream', 0, 0)  16.7 us
    ppermute x1, starting transfers between devices, body(): first_x = lax.ppermute(first_x, 'stream', pairing(count, 0))  8.93 us
    ppermute x1, starting transfers between devices, body(): first_z = lax.ppermute(first_z, 'span', pairing(spans, 0))  8.43 us
    pallas_call x1, Pallas kernels, body(): pl.pallas_call(functools.partial(local_kernel, (times, cx, cz, pairs, poi...  5.33 us
    pallas_call x1, Pallas kernels, body(): pl.pallas_call(functools.partial(finish_kernel, (times, cx, cz, pairs, po...  5.12 us
    ppermute x1, starting transfers between devices, body(): second_x = lax.ppermute(second_x, 'stream', pairing(count, 1))  3.35 us
    pallas_call x1, Pallas kernels, body(): pl.pallas_call(functools.partial(edge_kernel, (times, cx, cz, pairs)), ou...  2.72 us
    ppermute x1, starting transfers between devices, body(): second_z = lax.ppermute(second_z, 'span', pairing(spans, 1))  2.08 us
  transfers between devices with their start and end apart: 5, of which 0 were waited for; matrix products, arithmetic and copies ran while one was open for 0% of the time, Pallas kernels for 10%

profile of v2, /device:TPU:23, one launch (start us, length us, event | category | flops | bytes accessed | tf_op | source)
XLA Modules:
  0.0 56.0 jit_solution(3379924618806709366)
XLA Ops:
  0.0 0.0 copy-start
  0.0 0.0 copy-start.6
  0.0 0.0 copy-start.5
  0.0 0.0 copy-start.4
  0.0 0.0 copy-start.3
  0.0 0.0 copy-start.2
  0.0 2.7 %edges.1 = (bf16[64,16,128]{2,1,0:T(8,128)(2,1)}, bf16[48,1152]{1,0:T(8,128)(2,1)}, bf16[56,1152]{1,0:T(8,128)(2,1)}, bf16[48,1152]{1,0:T(8,128)(2,1)}, bf16[56,1152]{1,0:T(8,128)(2,1)}) custom-call(f32[336,1152]{1,0:T(8,128)} %bitcast.8), custom_call_target="tpu_custom_call" | custom-call | tf_op jit(solution)/shard_map/edges/pallas_call | solution.py:398
  2.8 16.7 %all-to-all-start = ((bf16[64,16,128]{2,1,0:T(8,128)(2,1)}), bf16[64,16,128]{2,1,0:T(8,128)(2,1)}, u32[]{:S(2)}, u32[]{:S(2)}) async-start(bf16[64,16,128]{2,1,0:T(8,128)(2,1)} %get-tuple-element.16), calls=%async_computation | async-start | bytes 524288 | tf_op jit(solution)/shard_map/all_to_all | solution.py:413
  19.5 3.4 %collective-permute-start.1 = (bf16[56,1152]{1,0:T(8,128)(2,1)}, bf16[56,1152]{1,0:T(8,128)(2,1)}, u32[]{:S(2)}, u32[]{:S(2)}) collective-permute-start(bf16[56,1152]{1,0:T(8,128)(2,1)} %get-tuple-element.24), channel_id=1, source_target_pairs={{8,16},{24,32},{40,48},{56,64},{72,80},{88,96},{104,112},{120,128}... | collective-permute-start | bytes 387080 | tf_op jit(solution)/shard_map/ppermute | solution.py:415
  22.9 8.9 %collective-permute-start.3 = (bf16[56,1152]{1,0:T(8,128)(2,1)}, bf16[56,1152]{1,0:T(8,128)(2,1)}, u32[]{:S(2)}, u32[]{:S(2)}) collective-permute-start(bf16[56,1152]{1,0:T(8,128)(2,1)} %get-tuple-element.26), channel_id=1, source_target_pairs={{0,8},{16,24},{32,40},{48,56},{64,72},{80,88},{96,104},{112,120},{... | collective-permute-start | bytes 387080 | tf_op jit(solution)/shard_map/ppermute | solution.py:416
  31.8 2.1 %collective-permute-start = (bf16[48,1152]{1,0:T(8,128)(2,1)}, bf16[48,1152]{1,0:T(8,128)(2,1)}, u32[]{:S(2)}, u32[]{:S(2)}) collective-permute-start(bf16[48,1152]{1,0:T(8,128)(2,1)} %get-tuple-element.23), channel_id=1, source_target_pairs={{1,2},{3,4},{5,6},{2,1},{4,3},{6,5},{9,10},{11,12},{13,14},{10,9},... | collective-permute-start | bytes 331784 | tf_op jit(solution)/shard_map/ppermute | solution.py:414
  33.9 8.4 %collective-permute-start.2 = (bf16[48,1152]{1,0:T(8,128)(2,1)}, bf16[48,1152]{1,0:T(8,128)(2,1)}, u32[]{:S(2)}, u32[]{:S(2)}) collective-permute-start(bf16[48,1152]{1,0:T(8,128)(2,1)} %get-tuple-element.25), channel_id=1, source_target_pairs={{0,1},{2,3},{4,5},{6,7},{1,0},{3,2},{5,4},{7,6},{8,9},{10,11},{12,... | collective-permute-start | bytes 331784 | tf_op jit(solution)/shard_map/ppermute | solution.py:417
  44.3 0.0 copy-done.6
  44.3 0.1 copy.11.owner_ref
  44.4 0.0 copy-done
  44.4 0.0 copy-done.5
  44.4 0.0 copy-done.4
  44.4 0.0 copy-done.3
  44.4 0.0 copy-done.2
  44.4 0.0 copy-start.1
  44.4 1.1 %copy-done.1 = bf16[7,6,8,1152]{3,2,1,0:T(8,128)(2,1)S(1)} copy-done((bf16[7,6,8,1152]{3,2,1,0:T(8,128)(2,1)S(1)}, bf16[7,6,8,1152]{3,2,1,0:T(8,128)(2,1)}, u32[]{:S(2)}) %copy-start.1) | copy-done | bytes 774168
  45.5 5.3 %local.1 = (f32[336,1152]{1,0:T(8,128)}, bf16[3,4,256,256]{3,2,1,0:T(8,128)(2,1)}, bf16[256,128]{1,0:T(8,128)(2,1)}, bf16[48,128]{1,0:T(8,128)(2,1)}, f32[48,128]{1,0:T(8,128)}, /*index=5*/f32[112,384]{1,0:T(8,128)}) custom-call(f32[1]{0:T(128)S(6)} %copy.12.omega_ref, f32[1]{0:T(128)S(6)} %copy.13.phase_ref, s32[1]{0:T(128)} %bitcast.6.live_ref, ...), custom_call_target="tpu_custom_call" | custom-call | flops 20000000 | bytes 6000000 | tf_op jit(solution)/shard_map/local/pallas_call | solution.py:422
  50.9 0.0 collective-permute-done.second_z_ref
  50.9 0.0 collective-permute-done.2.first_z_ref
  50.9 0.0 collective-permute-done.1.second_x_ref
  50.9 0.0 collective-permute-done.3.first_x_ref
  50.9 0.0 all-to-all-done.rim_ref
  50.9 5.1 %finish.1 = f32[336,1152]{1,0:T(8,128)} custom-call(s32[1]{0:T(128)} %bitcast.7.live_ref, bf16[64,16,128]{2,1,0:T(8,128)(2,1)} %all-to-all-done.rim_ref, f32[336,1152]{1,0:T(8,128)} %get-tuple-element.17.work_ref, bf16[3,4,256,256]{3,2,1,0:T(8,128)(2,1)} %get-tuple-element.18.green_ref, bf16[256,128]{1,0:T(8,128)(2,1)} %get-tuple-element.19.shift_ref, ...), custom_call_target="tpu_custom_call" | custom-call | flops 800000000 | bytes 5000000 | tf_op jit(solution)/shard_map/finish/pallas_call | solution.py:481
Async XLA Ops:
  0.0 44.4 %copy-start = (f32[7,6,8,1152]{3,2,1,0:T(8,128)S(1)}, f32[7,6,8,1152]{3,2,1,0:T(8,128)}, u32[]{:S(2)}) copy-start(f32[7,6,8,1152]{3,2,1,0:T(8,128)} %param.10) | copy-start | bytes 4644868
  0.0 44.3 %copy-start.6 = (s32[1,1,48,1]{2,3,1,0:T(1,128)S(1)}, s32[1,1,48,1]{2,3,1,0:T(1,128)}, u32[]{:S(2)}) copy-start(s32[1,1,48,1]{2,3,1,0:T(1,128)} %param.17) | copy-start | bytes 580
  0.0 44.4 %copy-start.5 = (s32[1,1,48]{2,1,0:T(1,128)S(1)}, s32[1,1,48]{2,1,0:T(1,128)}, u32[]{:S(2)}) copy-start(s32[1,1,48]{2,1,0:T(1,128)} %param.18) | copy-start | bytes 580
  0.0 44.4 %copy-start.4 = (f32[6,192]{1,0:T(8,128)S(1)}, f32[6,192]{1,0:T(8,128)}, u32[]{:S(2)}) copy-start(f32[6,192]{1,0:T(8,128)} %diag_ref.1) | copy-start | bytes 13828
  0.0 44.4 %copy-start.3 = (f32[6,192]{1,0:T(8,128)S(1)}, f32[6,192]{1,0:T(8,128)}, u32[]{:S(2)}) copy-start(f32[6,192]{1,0:T(8,128)} %coupling_ref.1) | copy-start | bytes 13828
  0.0 44.4 %copy-start.2 = (f32[6,8,768]{2,1,0:T(8,128)S(1)}, f32[6,8,768]{2,1,0:T(8,128)}, u32[]{:S(2)}) copy-start(f32[6,8,768]{2,1,0:T(8,128)} %param.12) | copy-start | bytes 442372
  2.8 48.1 %all-to-all-start = ((bf16[64,16,128]{2,1,0:T(8,128)(2,1)}), bf16[64,16,128]{2,1,0:T(8,128)(2,1)}, u32[]{:S(2)}, u32[]{:S(2)}) async-start(bf16[64,16,128]{2,1,0:T(8,128)(2,1)} %get-tuple-element.16), calls=%async_computation | async-start | bytes 524288 | tf_op jit(solution)/shard_map/all_to_all | solution.py:413
  19.5 31.4 %collective-permute-start.1 = (bf16[56,1152]{1,0:T(8,128)(2,1)}, bf16[56,1152]{1,0:T(8,128)(2,1)}, u32[]{:S(2)}, u32[]{:S(2)}) collective-permute-start(bf16[56,1152]{1,0:T(8,128)(2,1)} %get-tuple-element.24), channel_id=1, source_target_pairs={{8,16},{24,32},{40,48},{56,64},{72,80},{88,96},{104,112},{120,128}... | collective-permute-start | bytes 387080 | tf_op jit(solution)/shard_map/ppermute | solution.py:415
  22.9 28.0 %collective-permute-start.3 = (bf16[56,1152]{1,0:T(8,128)(2,1)}, bf16[56,1152]{1,0:T(8,128)(2,1)}, u32[]{:S(2)}, u32[]{:S(2)}) collective-permute-start(bf16[56,1152]{1,0:T(8,128)(2,1)} %get-tuple-element.26), channel_id=1, source_target_pairs={{0,8},{16,24},{32,40},{48,56},{64,72},{80,88},{96,104},{112,120},{... | collective-permute-start | bytes 387080 | tf_op jit(solution)/shard_map/ppermute | solution.py:416
  31.8 19.1 %collective-permute-start = (bf16[48,1152]{1,0:T(8,128)(2,1)}, bf16[48,1152]{1,0:T(8,128)(2,1)}, u32[]{:S(2)}, u32[]{:S(2)}) collective-permute-start(bf16[48,1152]{1,0:T(8,128)(2,1)} %get-tuple-element.23), channel_id=1, source_target_pairs={{1,2},{3,4},{5,6},{2,1},{4,3},{6,5},{9,10},{11,12},{13,14},{10,9},... | collective-permute-start | bytes 331784 | tf_op jit(solution)/shard_map/ppermute | solution.py:414
  33.9 17.0 %collective-permute-start.2 = (bf16[48,1152]{1,0:T(8,128)(2,1)}, bf16[48,1152]{1,0:T(8,128)(2,1)}, u32[]{:S(2)}, u32[]{:S(2)}) collective-permute-start(bf16[48,1152]{1,0:T(8,128)(2,1)} %get-tuple-element.25), channel_id=1, source_target_pairs={{0,1},{2,3},{4,5},{6,7},{1,0},{3,2},{5,4},{7,6},{8,9},{10,11},{12,... | collective-permute-start | bytes 331784 | tf_op jit(solution)/shard_map/ppermute | solution.py:417
  44.4 1.1 %copy-start.1 = (bf16[7,6,8,1152]{3,2,1,0:T(8,128)(2,1)S(1)}, bf16[7,6,8,1152]{3,2,1,0:T(8,128)(2,1)}, u32[]{:S(2)}) copy-start(bf16[7,6,8,1152]{3,2,1,0:T(8,128)(2,1)} %source_ref.1) | copy-start | bytes 2322436

commit v3 on v2

--- a/solution.py
+++ b/solution.py
@@ -100,7 +100,7 @@
     omega_ref,
     phase_ref,
     live_ref,
-    u_ref,
+    u_hbm,
     source_ref,
     stencil_ref,
     coupling_ref,
@@ -121,6 +121,8 @@
     sum_col,
     face_s,
     round_s,
+    u_s,
+    u_sems,
 ):
     times, cx, cz, pairs, points, count = dims
     rows = cx * cz
@@ -128,8 +130,16 @@
     pair_now = pl.program_id(0)
     wide = couple_s.shape[1]
 
+    trio = u_s.shape[2]
+
+    def fetch(pair):
+        lanes = pl.ds(pl.multiple_of(pair * trio, trio), trio)
+        return pltpu.make_async_copy(u_hbm.at[:, lanes], u_s.at[pair], u_sems.at[pair])
+
     @pl.when(pair_now == 0)
     def prepare():
+        for pair in range(pairs):
+            fetch(pair).start()
         states = coupling_ref.shape[0]
         lane = iota((8, wide), 1)
         couple_s[...] = jnp.ones_like(couple_s)
@@ -249,6 +259,8 @@
         green_ref[0, 2 * half] = high
         green_ref[0, 2 * half + 1] = low_part
 
+    fetch(pair_now).wait()
+    u_ref = u_s.at[pair_now]
     round_s[...] = u_ref[...].astype(BF16).astype(F32)
     omega = omega_ref[0]
     live = live_ref[0]
@@ -434,7 +446,7 @@
             smem,
             smem,
             smem,
-            pl.BlockSpec((lines, trio), lambda p: (0, p)),
+            pl.BlockSpec(memory_space=pltpu.HBM),
             pl.BlockSpec((times, cx, cz, trio), lambda p: (0, 0, 0, p)),
             pl.BlockSpec((rows, 4 * points), lambda p: (0, 0)),
             pl.BlockSpec((states, points), lambda p: (0, 0)),
@@ -459,8 +471,10 @@
             pltpu.VMEM((wide, 8), F32),
             pltpu.VMEM((4 * rows, trio), F32),
             pltpu.VMEM((lines, trio), F32),
+            pltpu.VMEM((pairs, lines, trio), F32),
+            pltpu.SemaphoreType.DMA((pairs,)),
         ],
-        compiler_params=pltpu.CompilerParams(vmem_limit_bytes=16 * 2**20),
+        compiler_params=pltpu.CompilerParams(vmem_limit_bytes=52 * 2**20),
         cost_estimate=pl.CostEstimate(flops=20_000_000, bytes_accessed=6_000_000, transcendentals=400_000),
         name="local",
     )(

time: 56.4 us -> 55.6 us (0.986)
  local copies, waits for them, and re-layouts: 1.24 us -> 0.12 us
    unnamed x14 -> x12, local copies, waits for them, and re-layouts: 1.15 us -> 0.02 us
where the time goes in v3:
time: 55.6 us; the launch traced here: 55.2 us
  starting transfers between devices  39.5 us (71%)
  Pallas kernels  13.5 us (24%)
  between operations  2.09 us (4%)
    all_to_all x1, starting transfers between devices, body(): rims = lax.all_to_all(rim, 'stream', 0, 0)  16.7 us
    ppermute x1, starting transfers between devices, body(): first_x = lax.ppermute(first_x, 'stream', pairing(count, 0))  8.93 us
    ppermute x1, starting transfers between devices, body(): first_z = lax.ppermute(first_z, 'span', pairing(spans, 0))  8.43 us
    pallas_call x1, Pallas kernels, body(): pl.pallas_call(functools.partial(local_kernel, (times, cx, cz, pairs, poi...  5.68 us
    pallas_call x1, Pallas kernels, body(): pl.pallas_call(functools.partial(finish_kernel, (times, cx, cz, pairs, po...  5.12 us
    ppermute x1, starting transfers between devices, body(): second_x = lax.ppermute(second_x, 'stream', pairing(count, 1))  3.35 us
    pallas_call x1, Pallas kernels, body(): pl.pallas_call(functools.partial(edge_kernel, (times, cx, cz, pairs)), ou...  2.67 us
    ppermute x1, starting transfers between devices, body(): second_z = lax.ppermute(second_z, 'span', pairing(spans, 1))  2.08 us
  transfers between devices with their start and end apart: 5, of which 0 were waited for; matrix products, arithmetic and copies ran while one was open for 0% of the time, Pallas kernels for 10%

profile of v3, /device:TPU:23, one launch (start us, length us, event | category | flops | bytes accessed | tf_op | source)
XLA Modules:
  0.0 55.2 jit_solution(8553345554603555129)
XLA Ops:
  0.0 0.0 copy-start.5
  0.0 0.0 copy-start.4
  0.0 0.0 copy-start.3
  0.0 0.0 copy-start.2
  0.0 0.0 copy-start.1
  0.0 0.0 copy-start
  0.0 2.7 %edges.1 = (bf16[64,16,128]{2,1,0:T(8,128)(2,1)}, bf16[48,1152]{1,0:T(8,128)(2,1)}, bf16[56,1152]{1,0:T(8,128)(2,1)}, bf16[48,1152]{1,0:T(8,128)(2,1)}, bf16[56,1152]{1,0:T(8,128)(2,1)}) custom-call(f32[336,1152]{1,0:T(8,128)} %bitcast.10), custom_call_target="tpu_custom_call" | custom-call | tf_op jit(solution)/shard_map/edges/pallas_call | solution.py:410
  2.7 16.7 %all-to-all-start = ((bf16[64,16,128]{2,1,0:T(8,128)(2,1)}), bf16[64,16,128]{2,1,0:T(8,128)(2,1)}, u32[]{:S(2)}, u32[]{:S(2)}) async-start(bf16[64,16,128]{2,1,0:T(8,128)(2,1)} %get-tuple-element.16), calls=%async_computation | async-start | bytes 524288 | tf_op jit(solution)/shard_map/all_to_all | solution.py:425
  19.5 3.4 %collective-permute-start.1 = (bf16[56,1152]{1,0:T(8,128)(2,1)}, bf16[56,1152]{1,0:T(8,128)(2,1)}, u32[]{:S(2)}, u32[]{:S(2)}) collective-permute-start(bf16[56,1152]{1,0:T(8,128)(2,1)} %get-tuple-element.24), channel_id=1, source_target_pairs={{8,16},{24,32},{40,48},{56,64},{72,80},{88,96},{104,112},{120,128}... | collective-permute-start | bytes 387080 | tf_op jit(solution)/shard_map/ppermute | solution.py:427
  22.8 8.9 %collective-permute-start.3 = (bf16[56,1152]{1,0:T(8,128)(2,1)}, bf16[56,1152]{1,0:T(8,128)(2,1)}, u32[]{:S(2)}, u32[]{:S(2)}) collective-permute-start(bf16[56,1152]{1,0:T(8,128)(2,1)} %get-tuple-element.26), channel_id=1, source_target_pairs={{0,8},{16,24},{32,40},{48,56},{64,72},{80,88},{96,104},{112,120},{... | collective-permute-start | bytes 387080 | tf_op jit(solution)/shard_map/ppermute | solution.py:428
  31.7 2.1 %collective-permute-start = (bf16[48,1152]{1,0:T(8,128)(2,1)}, bf16[48,1152]{1,0:T(8,128)(2,1)}, u32[]{:S(2)}, u32[]{:S(2)}) collective-permute-start(bf16[48,1152]{1,0:T(8,128)(2,1)} %get-tuple-element.23), channel_id=1, source_target_pairs={{1,2},{3,4},{5,6},{2,1},{4,3},{6,5},{9,10},{11,12},{13,14},{10,9},... | collective-permute-start | bytes 331784 | tf_op jit(solution)/shard_map/ppermute | solution.py:426
  33.8 8.4 %collective-permute-start.2 = (bf16[48,1152]{1,0:T(8,128)(2,1)}, bf16[48,1152]{1,0:T(8,128)(2,1)}, u32[]{:S(2)}, u32[]{:S(2)}) collective-permute-start(bf16[48,1152]{1,0:T(8,128)(2,1)} %get-tuple-element.25), channel_id=1, source_target_pairs={{0,1},{2,3},{4,5},{6,7},{1,0},{3,2},{5,4},{7,6},{8,9},{10,11},{12,... | collective-permute-start | bytes 331784 | tf_op jit(solution)/shard_map/ppermute | solution.py:429
  44.2 0.0 copy-done.5
  44.2 0.1 copy.11.owner_ref
  44.3 0.0 copy-done.4
  44.3 0.0 copy-done.3
  44.3 0.0 copy-done.2
  44.3 0.0 copy-done.1
  44.3 0.0 copy-done
  44.4 5.7 %local.1 = (f32[336,1152]{1,0:T(8,128)}, bf16[3,4,256,256]{3,2,1,0:T(8,128)(2,1)}, bf16[256,128]{1,0:T(8,128)(2,1)}, bf16[48,128]{1,0:T(8,128)(2,1)}, f32[48,128]{1,0:T(8,128)}, /*index=5*/f32[112,384]{1,0:T(8,128)}) custom-call(f32[1]{0:T(128)S(6)} %copy.12.omega_ref, f32[1]{0:T(128)S(6)} %copy.13.phase_ref, s32[1]{0:T(128)} %bitcast.6.live_ref, ...), custom_call_target="tpu_custom_call" | custom-call | flops 20000000 | bytes 6000000 | tf_op jit(solution)/shard_map/local/pallas_call | solution.py:434
  50.0 0.0 collective-permute-done.second_z_ref
  50.1 0.0 collective-permute-done.2.first_z_ref
  50.1 0.0 collective-permute-done.1.second_x_ref
  50.1 0.0 collective-permute-done.3.first_x_ref
  50.1 0.0 all-to-all-done.rim_ref
  50.1 5.1 %finish.1 = f32[336,1152]{1,0:T(8,128)} custom-call(s32[1]{0:T(128)} %bitcast.7.live_ref, bf16[64,16,128]{2,1,0:T(8,128)(2,1)} %all-to-all-done.rim_ref, f32[336,1152]{1,0:T(8,128)} %get-tuple-element.17.work_ref, bf16[3,4,256,256]{3,2,1,0:T(8,128)(2,1)} %get-tuple-element.18.green_ref, bf16[256,128]{1,0:T(8,128)(2,1)} %get-tuple-element.19.shift_ref, ...), custom_call_target="tpu_custom_call" | custom-call | flops 800000000 | bytes 5000000 | tf_op jit(solution)/shard_map/finish/pallas_call | solution.py:495
Async XLA Ops:
  0.0 44.2 %copy-start.5 = (s32[1,1,48,1]{2,3,1,0:T(1,128)S(1)}, s32[1,1,48,1]{2,3,1,0:T(1,128)}, u32[]{:S(2)}) copy-start(s32[1,1,48,1]{2,3,1,0:T(1,128)} %param.17) | copy-start | bytes 580
  0.0 44.3 %copy-start.4 = (s32[1,1,48]{2,1,0:T(1,128)S(1)}, s32[1,1,48]{2,1,0:T(1,128)}, u32[]{:S(2)}) copy-start(s32[1,1,48]{2,1,0:T(1,128)} %param.18) | copy-start | bytes 580
  0.0 44.3 %copy-start.3 = (f32[6,192]{1,0:T(8,128)S(1)}, f32[6,192]{1,0:T(8,128)}, u32[]{:S(2)}) copy-start(f32[6,192]{1,0:T(8,128)} %diag_ref.1) | copy-start | bytes 13828
  0.0 44.3 %copy-start.2 = (f32[6,192]{1,0:T(8,128)S(1)}, f32[6,192]{1,0:T(8,128)}, u32[]{:S(2)}) copy-start(f32[6,192]{1,0:T(8,128)} %coupling_ref.1) | copy-start | bytes 13828
  0.0 44.3 %copy-start.1 = (f32[6,8,768]{2,1,0:T(8,128)S(1)}, f32[6,8,768]{2,1,0:T(8,128)}, u32[]{:S(2)}) copy-start(f32[6,8,768]{2,1,0:T(8,128)} %param.12) | copy-start | bytes 442372
  0.0 44.3 %copy-start = (bf16[7,6,8,1152]{3,2,1,0:T(8,128)(2,1)S(1)}, bf16[7,6,8,1152]{3,2,1,0:T(8,128)(2,1)}, u32[]{:S(2)}) copy-start(bf16[7,6,8,1152]{3,2,1,0:T(8,128)(2,1)} %source_ref.1) | copy-start | bytes 2322436
  2.7 47.4 %all-to-all-start = ((bf16[64,16,128]{2,1,0:T(8,128)(2,1)}), bf16[64,16,128]{2,1,0:T(8,128)(2,1)}, u32[]{:S(2)}, u32[]{:S(2)}) async-start(bf16[64,16,128]{2,1,0:T(8,128)(2,1)} %get-tuple-element.16), calls=%async_computation | async-start | bytes 524288 | tf_op jit(solution)/shard_map/all_to_all | solution.py:425
  19.5 30.6 %collective-permute-start.1 = (bf16[56,1152]{1,0:T(8,128)(2,1)}, bf16[56,1152]{1,0:T(8,128)(2,1)}, u32[]{:S(2)}, u32[]{:S(2)}) collective-permute-start(bf16[56,1152]{1,0:T(8,128)(2,1)} %get-tuple-element.24), channel_id=1, source_target_pairs={{8,16},{24,32},{40,48},{56,64},{72,80},{88,96},{104,112},{120,128}... | collective-permute-start | bytes 387080 | tf_op jit(solution)/shard_map/ppermute | solution.py:427
  22.8 27.3 %collective-permute-start.3 = (bf16[56,1152]{1,0:T(8,128)(2,1)}, bf16[56,1152]{1,0:T(8,128)(2,1)}, u32[]{:S(2)}, u32[]{:S(2)}) collective-permute-start(bf16[56,1152]{1,0:T(8,128)(2,1)} %get-tuple-element.26), channel_id=1, source_target_pairs={{0,8},{16,24},{32,40},{48,56},{64,72},{80,88},{96,104},{112,120},{... | collective-permute-start | bytes 387080 | tf_op jit(solution)/shard_map/ppermute | solution.py:428
  31.7 18.3 %collective-permute-start = (bf16[48,1152]{1,0:T(8,128)(2,1)}, bf16[48,1152]{1,0:T(8,128)(2,1)}, u32[]{:S(2)}, u32[]{:S(2)}) collective-permute-start(bf16[48,1152]{1,0:T(8,128)(2,1)} %get-tuple-element.23), channel_id=1, source_target_pairs={{1,2},{3,4},{5,6},{2,1},{4,3},{6,5},{9,10},{11,12},{13,14},{10,9},... | collective-permute-start | bytes 331784 | tf_op jit(solution)/shard_map/ppermute | solution.py:426
  33.8 16.2 %collective-permute-start.2 = (bf16[48,1152]{1,0:T(8,128)(2,1)}, bf16[48,1152]{1,0:T(8,128)(2,1)}, u32[]{:S(2)}, u32[]{:S(2)}) collective-permute-start(bf16[48,1152]{1,0:T(8,128)(2,1)} %get-tuple-element.25), channel_id=1, source_target_pairs={{0,1},{2,3},{4,5},{6,7},{1,0},{3,2},{5,4},{7,6},{8,9},{10,11},{12,... | collective-permute-start | bytes 331784 | tf_op jit(solution)/shard_map/ppermute | solution.py:429

commit v4 on v3

--- a/solution.py
+++ b/solution.py
@@ -28,17 +28,31 @@
     return high, (value - high.astype(F32)).astype(BF16)
 
 
-def edge_kernel(dims, u_ref, rim_ref, second_z_ref, second_x_ref, first_z_ref, first_x_ref):
+def edge_kernel(
+    dims, u_hbm, rim_ref, second_z_ref, second_x_ref, first_z_ref, first_x_ref, u_ref, u_sems
+):
     times, cx, cz, pairs = dims
     rows = cx * cz
-    width = u_ref.shape[1]
+    trio = u_ref.shape[1] // pairs
+    spans = [slice(pair * trio, (pair + 1) * trio) for pair in range(pairs)]
+    fetches = [
+        pltpu.make_async_copy(u_hbm.at[:, lanes], u_ref.at[:, lanes], u_sems.at[pair])
+        for pair, lanes in enumerate(spans)
+    ]
+    for fetch in fetches:
+        fetch.start()
+    even_x = lax.axis_index("stream") % 2 == 0
+    even_z = lax.axis_index("span") % 2 == 0
+    top = cz - 1
+    sub = iota((8, trio), 0)
     lane = iota((rows, LANES), 1)
     inner = lane % HALF
     span = times * pairs
     found = jnp.zeros((rows, LANES), F32)
-    for t in range(times):
-        for pair in range(pairs):
-            base = pair * 3 * LANES
+    for pair, lanes in enumerate(spans):
+        fetches[pair].wait()
+        base = pair * trio
+        for t in range(times):
             block = slice(t * rows, (t + 1) * rows)
             first = u_ref[block, base + LANES : base + 2 * LANES]
             second = u_ref[block, base + 2 * LANES : base + 3 * LANES]
@@ -46,6 +60,22 @@
             spot = t * pairs + pair
             both = pltpu.roll(both, (spot - (HALF - 1)) % LANES, 1)
             found = jnp.where(inner == spot, both, found)
+        take = lambda t, x: u_ref[t * rows + x * cz : t * rows + x * cz + cz, lanes]
+        west = jnp.concatenate([take(t, 0) for t in range(times)], 0)
+        east = jnp.concatenate([take(t, cx - 1) for t in range(times)], 0)
+        first_x_ref[:, lanes] = jnp.where(even_x, east, west).astype(BF16)
+        second_x_ref[:, lanes] = jnp.where(even_x, west, east).astype(BF16)
+        for ref, z in (
+            (first_z_ref, jnp.where(even_z, top, 0)),
+            (second_z_ref, jnp.where(even_z, 0, top)),
+        ):
+            tiles = []
+            for x in range(cx):
+                tile = jnp.zeros((8, trio), F32)
+                for t in range(times):
+                    tile = jnp.where(sub == t, u_ref[pl.ds(t * rows + x * cz + z, 1), lanes], tile)
+                tiles.append(tile)
+            ref[:, lanes] = jnp.concatenate(tiles, 0).astype(BF16)
     part = rows // GROUPS
     parts = []
     for _ in range(PARTS):
@@ -58,24 +88,6 @@
     packed = jnp.concatenate(parts, 0).astype(BF16)
     for other in range(rim_ref.shape[0]):
         rim_ref[other] = packed
-
-    take = lambda t, x: u_ref[t * rows + x * cz : t * rows + x * cz + cz, :]
-    west = jnp.concatenate([take(t, 0) for t in range(times)], 0)
-    east = jnp.concatenate([take(t, cx - 1) for t in range(times)], 0)
-    even_x = lax.axis_index("stream") % 2 == 0
-    first_x_ref[...] = jnp.where(even_x, east, west).astype(BF16)
-    second_x_ref[...] = jnp.where(even_x, west, east).astype(BF16)
-    sub = iota((8, width), 0)
-    even_z = lax.axis_index("span") % 2 == 0
-    top = cz - 1
-    for ref, z in ((first_z_ref, jnp.where(even_z, top, 0)), (second_z_ref, jnp.where(even_z, 0, top))):
-        tiles = []
-        for x in range(cx):
-            tile = jnp.zeros((8, width), F32)
-            for t in range(times):
-                tile = jnp.where(sub == t, u_ref[pl.ds(t * rows + x * cz + z, 1), :], tile)
-            tiles.append(tile)
-        ref[...] = jnp.concatenate(tiles, 0).astype(BF16)
 
 
 def scan_products(matrix, lane, points, backward):
@@ -108,17 +120,16 @@
     owner_ref,
     row_ref,
     work_ref,
-    green_ref,
+    couple_s,
+    green_row,
+    sum_row,
+    green_col,
+    sum_col,
     shift_ref,
     pick_ref,
     keep_ref,
     rimw_ref,
-    couple_s,
     diag_s,
-    green_row,
-    sum_row,
-    green_col,
-    sum_col,
     face_s,
     round_s,
     u_s,
@@ -232,33 +243,6 @@
         shift_ref[0:LANES, :] = high
         shift_ref[LANES : 2 * LANES, :] = low_part
 
-    for half in range(2):
-        state = 2 * pair_now + half
-        first = half * HALF
-        g_row = green_row[pl.ds(state, 1), :]
-        s_row = sum_row[pl.ds(state, 1), :]
-        pick = iota((wide, 8), 1) == state
-        g_col = jnp.sum(jnp.where(pick, green_col[...], 0.0), axis=1, keepdims=True)
-        s_col = jnp.sum(jnp.where(pick, sum_col[...], 0.0), axis=1, keepdims=True)
-        k = iota((wide, wide), 0)
-        n = iota((wide, wide), 1)
-        full = jnp.exp(-jnp.abs(s_col - s_row)) * jnp.where(k <= n, g_col, g_row)
-        at_end = first + points - 1
-        lane = iota((1, wide), 1)
-        s_end = jnp.sum(jnp.where(lane == at_end, s_row, 0.0), axis=1, keepdims=True)
-        link = couple_s[pl.ds(state, 1), :]
-        c_end = jnp.sum(jnp.where(lane == points - 1, link, 0.0), axis=1, keepdims=True)
-        last = c_end * jnp.exp(-jnp.abs(s_end - s_row)) * g_row
-        inside_k = (k >= first) & (k < first + points)
-        inside_n = (n >= first) & (n < first + points)
-        inner = k % HALF
-        added = (inner < span) & (inner % pairs == pair_now)
-        full = jnp.where(inside_k, full, jnp.where(added, last, 0.0))
-        full = jnp.where(inside_n, full, 0.0)
-        high, low_part = split(full)
-        green_ref[0, 2 * half] = high
-        green_ref[0, 2 * half + 1] = low_part
-
     fetch(pair_now).wait()
     u_ref = u_s.at[pair_now]
     round_s[...] = u_ref[...].astype(BF16).astype(F32)
@@ -291,7 +275,11 @@
     live_ref,
     rim_ref,
     work_ref,
-    green_ref,
+    couple_s,
+    green_row,
+    sum_row,
+    green_col,
+    sum_col,
     shift_ref,
     pick_ref,
     keep_ref,
@@ -360,12 +348,41 @@
             high, low = split(jnp.concatenate(pieces, 0))
             high_s[half, t * rows : (t + 1) * rows, :] = high
             low_s[half, t * rows : (t + 1) * rows, :] = low
+    pair_now = pl.program_id(0)
+    span = times * pairs
+    wide = couple_s.shape[1]
+    inverses = []
+    for half in range(2):
+        state = 2 * pair_now + half
+        first = half * HALF
+        g_row = green_row[pl.ds(state, 1), :]
+        s_row = sum_row[pl.ds(state, 1), :]
+        pick = iota((wide, 8), 1) == state
+        g_col = jnp.sum(jnp.where(pick, green_col[...], 0.0), axis=1, keepdims=True)
+        s_col = jnp.sum(jnp.where(pick, sum_col[...], 0.0), axis=1, keepdims=True)
+        k = iota((wide, wide), 0)
+        n = iota((wide, wide), 1)
+        full = jnp.exp(-jnp.abs(s_col - s_row)) * jnp.where(k <= n, g_col, g_row)
+        at_end = first + points - 1
+        lane = iota((1, wide), 1)
+        s_end = jnp.sum(jnp.where(lane == at_end, s_row, 0.0), axis=1, keepdims=True)
+        link = couple_s[pl.ds(state, 1), :]
+        c_end = jnp.sum(jnp.where(lane == points - 1, link, 0.0), axis=1, keepdims=True)
+        last = c_end * jnp.exp(-jnp.abs(s_end - s_row)) * g_row
+        inside_k = (k >= first) & (k < first + points)
+        inside_n = (n >= first) & (n < first + points)
+        spot = k % HALF
+        added = (spot < span) & (spot % pairs == pair_now)
+        full = jnp.where(inside_k, full, jnp.where(added, last, 0.0))
+        full = jnp.where(inside_n, full, 0.0)
+        high, low_part = split(full)
+        inverses.append((high, low_part))
     products = []
     for half in range(2):
         high = high_s[half]
-        g_high = green_ref[0, 2 * half]
+        g_high, g_low = inverses[half]
         total = jnp.dot(high, g_high, preferred_element_type=F32)
-        total += jnp.dot(high, green_ref[0, 2 * half + 1], preferred_element_type=F32)
+        total += jnp.dot(high, g_low, preferred_element_type=F32)
         total += jnp.dot(low_s[half], g_high, preferred_element_type=F32)
         products.append(total)
     even, odd = products
@@ -416,8 +433,9 @@
             jax.ShapeDtypeStruct((cx * 8, width), BF16),
             jax.ShapeDtypeStruct((times * cz, width), BF16),
         ),
-        in_specs=[vmem],
+        in_specs=[pl.BlockSpec(memory_space=pltpu.HBM)],
         out_specs=(vmem,) * 5,
+        scratch_shapes=[pltpu.VMEM((lines, width), F32), pltpu.SemaphoreType.DMA((pairs,))],
         compiler_params=pltpu.CompilerParams(vmem_limit_bytes=VMEM_GRANT),
         name="edges",
     )(u)
@@ -431,11 +449,15 @@
     live = tile_live.reshape(1)
     trio = 3 * LANES
     rim_rows = 2 * cz + 2 * rows
-    work, green, shift, pick, keep, rim_weights = pl.pallas_call(
+    work, couple, green_row, sum_row, green_col, sum_col, shift, pick, keep, rim_weights = pl.pallas_call(
         functools.partial(local_kernel, (times, cx, cz, pairs, points, count)),
         out_shape=(
             pltpu.HBM((lines, width), F32),
-            pltpu.HBM((pairs, 4, wide, wide), BF16),
+            pltpu.HBM((8, wide), F32),
+            pltpu.HBM((8, wide), F32),
+            pltpu.HBM((8, wide), F32),
+            pltpu.HBM((wide, 8), F32),
+            pltpu.HBM((wide, 8), F32),
             pltpu.HBM((2 * LANES, LANES), BF16),
             pltpu.HBM((rows, OWNERS * part), BF16),
             pltpu.HBM((rows, LANES), F32),
@@ -456,7 +478,11 @@
         ],
         out_specs=(
             pl.BlockSpec((lines, trio), lambda p: (0, p)),
-            pl.BlockSpec((1, 4, wide, wide), lambda p: (p, 0, 0, 0)),
+            pl.BlockSpec((8, wide), lambda p: (0, 0)),
+            pl.BlockSpec((8, wide), lambda p: (0, 0)),
+            pl.BlockSpec((8, wide), lambda p: (0, 0)),
+            pl.BlockSpec((wide, 8), lambda p: (0, 0)),
+            pl.BlockSpec((wide, 8), lambda p: (0, 0)),
             pl.BlockSpec((2 * LANES, LANES), lambda p: (0, 0)),
             pl.BlockSpec((rows, OWNERS * part), lambda p: (0, 0)),
             pl.BlockSpec((rows, LANES), lambda p: (0, 0)),
@@ -464,11 +490,6 @@
         ),
         scratch_shapes=[
             pltpu.VMEM((8, wide), F32),
-            pltpu.VMEM((8, wide), F32),
-            pltpu.VMEM((8, wide), F32),
-            pltpu.VMEM((8, wide), F32),
-            pltpu.VMEM((wide, 8), F32),
-            pltpu.VMEM((wide, 8), F32),
             pltpu.VMEM((4 * rows, trio), F32),
             pltpu.VMEM((lines, trio), F32),
             pltpu.VMEM((pairs, lines, trio), F32),
@@ -500,7 +521,11 @@
             smem,
             pl.BlockSpec(rims.shape, lambda p: (0, 0, 0)),
             edge(work),
-            pl.BlockSpec((1, 4, wide, wide), lambda p: (p, 0, 0, 0)),
+            pl.BlockSpec((8, wide), lambda p: (0, 0)),
+            pl.BlockSpec((8, wide), lambda p: (0, 0)),
+            pl.BlockSpec((8, wide), lambda p: (0, 0)),
+            pl.BlockSpec((wide, 8), lambda p: (0, 0)),
+            pl.BlockSpec((wide, 8), lambda p: (0, 0)),
             whole(shift),
             whole(pick),
             whole(keep),
@@ -526,7 +551,11 @@
         live,
         rims,
         work,
-        green,
+        couple,
+        green_row,
+        sum_row,
+        green_col,
+        sum_col,
         shift,
         pick,
         keep,

time: 55.6 us -> 55.4 us (level)
  no operation moved by 1% of the time
where the time goes in v4:
time: 55.4 us; the launch traced here: 55.1 us
  starting transfers between devices  39.5 us (71%)
  Pallas kernels  13.3 us (24%)
  between operations  2.1 us (4%)
    all_to_all x1, starting transfers between devices, body(): rims = lax.all_to_all(rim, 'stream', 0, 0)  16.7 us
    ppermute x1, starting transfers between devices, body(): first_x = lax.ppermute(first_x, 'stream', pairing(count, 0))  8.93 us
    ppermute x1, starting transfers between devices, body(): first_z = lax.ppermute(first_z, 'span', pairing(spans, 0))  8.43 us
    pallas_call x1, Pallas kernels, body(): pl.pallas_call(functools.partial(local_kernel, (times, cx, cz, pairs, poi...  5.5 us
    pallas_call x1, Pallas kernels, body(): pl.pallas_call(functools.partial(finish_kernel, (times, cx, cz, pairs, po...  5.22 us
    ppermute x1, starting transfers between devices, body(): second_x = lax.ppermute(second_x, 'stream', pairing(count, 1))  3.35 us
    pallas_call x1, Pallas kernels, body(): pl.pallas_call(functools.partial(edge_kernel, (times, cx, cz, pairs)), ou...  2.56 us
    ppermute x1, starting transfers between devices, body(): second_z = lax.ppermute(second_z, 'span', pairing(spans, 1))  2.08 us
  transfers between devices with their start and end apart: 5, of which 0 were waited for; matrix products, arithmetic and copies ran while one was open for 0% of the time, Pallas kernels for 10%

profile of v4, /device:TPU:23, one launch (start us, length us, event | category | flops | bytes accessed | tf_op | source)
XLA Modules:
  0.0 55.1 jit_solution(17332823451500788244)
XLA Ops:
  0.0 0.0 copy-start.5
  0.0 0.0 copy-start.4
  0.0 0.0 copy-start.3
  0.0 0.0 copy-start.2
  0.0 0.0 copy-start.1
  0.0 0.0 copy-start
  0.0 2.6 %edges.1 = (bf16[64,16,128]{2,1,0:T(8,128)(2,1)}, bf16[48,1152]{1,0:T(8,128)(2,1)}, bf16[56,1152]{1,0:T(8,128)(2,1)}, bf16[48,1152]{1,0:T(8,128)(2,1)}, bf16[56,1152]{1,0:T(8,128)(2,1)}) custom-call(f32[336,1152]{1,0:T(8,128)} %bitcast.10), custom_call_target="tpu_custom_call" | custom-call | tf_op jit(solution)/shard_map/edges/pallas_call | solution.py:427
  2.6 16.7 %all-to-all-start = ((bf16[64,16,128]{2,1,0:T(8,128)(2,1)}), bf16[64,16,128]{2,1,0:T(8,128)(2,1)}, u32[]{:S(2)}, u32[]{:S(2)}) async-start(bf16[64,16,128]{2,1,0:T(8,128)(2,1)} %get-tuple-element.20), calls=%async_computation | async-start | bytes 524288 | tf_op jit(solution)/shard_map/all_to_all | solution.py:443
  19.4 3.4 %collective-permute-start.1 = (bf16[56,1152]{1,0:T(8,128)(2,1)}, bf16[56,1152]{1,0:T(8,128)(2,1)}, u32[]{:S(2)}, u32[]{:S(2)}) collective-permute-start(bf16[56,1152]{1,0:T(8,128)(2,1)} %get-tuple-element.32), channel_id=1, source_target_pairs={{8,16},{24,32},{40,48},{56,64},{72,80},{88,96},{104,112},{120,128}... | collective-permute-start | bytes 387080 | tf_op jit(solution)/shard_map/ppermute | solution.py:445
  22.7 8.9 %collective-permute-start.3 = (bf16[56,1152]{1,0:T(8,128)(2,1)}, bf16[56,1152]{1,0:T(8,128)(2,1)}, u32[]{:S(2)}, u32[]{:S(2)}) collective-permute-start(bf16[56,1152]{1,0:T(8,128)(2,1)} %get-tuple-element.34), channel_id=1, source_target_pairs={{0,8},{16,24},{32,40},{48,56},{64,72},{80,88},{96,104},{112,120},{... | collective-permute-start | bytes 387080 | tf_op jit(solution)/shard_map/ppermute | solution.py:446
  31.7 2.1 %collective-permute-start = (bf16[48,1152]{1,0:T(8,128)(2,1)}, bf16[48,1152]{1,0:T(8,128)(2,1)}, u32[]{:S(2)}, u32[]{:S(2)}) collective-permute-start(bf16[48,1152]{1,0:T(8,128)(2,1)} %get-tuple-element.31), channel_id=1, source_target_pairs={{1,2},{3,4},{5,6},{2,1},{4,3},{6,5},{9,10},{11,12},{13,14},{10,9},... | collective-permute-start | bytes 331784 | tf_op jit(solution)/shard_map/ppermute | solution.py:444
  33.7 8.4 %collective-permute-start.2 = (bf16[48,1152]{1,0:T(8,128)(2,1)}, bf16[48,1152]{1,0:T(8,128)(2,1)}, u32[]{:S(2)}, u32[]{:S(2)}) collective-permute-start(bf16[48,1152]{1,0:T(8,128)(2,1)} %get-tuple-element.33), channel_id=1, source_target_pairs={{0,1},{2,3},{4,5},{6,7},{1,0},{3,2},{5,4},{7,6},{8,9},{10,11},{12,... | collective-permute-start | bytes 331784 | tf_op jit(solution)/shard_map/ppermute | solution.py:447
  44.1 0.0 copy-done.5
  44.1 0.1 copy.11.owner_ref
  44.2 0.0 copy-done.4
  44.2 0.0 copy-done.3
  44.2 0.0 copy-done.2
  44.2 0.0 copy-done.1
  44.3 0.0 copy-done
  44.3 5.5 %local.1 = (f32[336,1152]{1,0:T(8,128)}, f32[8,256]{1,0:T(8,128)}, f32[8,256]{1,0:T(8,128)}, f32[8,256]{1,0:T(8,128)}, f32[256,8]{1,0:T(8,128)}, /*index=5*/f32[...) custom-call(f32[1]{0:T(128)S(6)} %copy.12.omega_ref, ...), custom_call_target="tpu_custom_call" | custom-call | flops 20000000 | bytes 6000000 | tf_op jit(solution)/shard_map/local/pallas_call | solution.py:452
  49.8 0.0 collective-permute-done.second_z_ref
  49.8 0.0 collective-permute-done.2.first_z_ref
  49.8 0.0 collective-permute-done.1.second_x_ref
  49.8 0.0 collective-permute-done.3.first_x_ref
  49.8 0.0 all-to-all-done.rim_ref
  49.8 5.2 %finish.1 = f32[336,1152]{1,0:T(8,128)} custom-call(s32[1]{0:T(128)} %bitcast.7.live_ref, bf16[64,16,128]{2,1,0:T(8,128)(2,1)} %all-to-all-done.rim_ref, f32[336,1152]{1,0:T(8,128)} %get-tuple-element.21.work_ref, f32[8,256]{1,0:T(8,128)} %get-tuple-element.22.couple_s, f32[8,256]{1,0:T(8,128)} %get-tuple-element.23.green_row, ...), custom_call_target="tpu_custom_call" | custom-call | flops 800000000 | bytes 5000000 | tf_op jit(solution)/shard_map/finish/pallas_call | solution.py:516
Async XLA Ops:
  0.0 44.1 %copy-start.5 = (s32[1,1,48,1]{2,3,1,0:T(1,128)S(1)}, s32[1,1,48,1]{2,3,1,0:T(1,128)}, u32[]{:S(2)}) copy-start(s32[1,1,48,1]{2,3,1,0:T(1,128)} %param.17) | copy-start | bytes 580
  0.0 44.2 %copy-start.4 = (s32[1,1,48]{2,1,0:T(1,128)S(1)}, s32[1,1,48]{2,1,0:T(1,128)}, u32[]{:S(2)}) copy-start(s32[1,1,48]{2,1,0:T(1,128)} %param.18) | copy-start | bytes 580
  0.0 44.2 %copy-start.3 = (f32[6,192]{1,0:T(8,128)S(1)}, f32[6,192]{1,0:T(8,128)}, u32[]{:S(2)}) copy-start(f32[6,192]{1,0:T(8,128)} %diag_ref.1) | copy-start | bytes 13828
  0.0 44.2 %copy-start.2 = (f32[6,192]{1,0:T(8,128)S(1)}, f32[6,192]{1,0:T(8,128)}, u32[]{:S(2)}) copy-start(f32[6,192]{1,0:T(8,128)} %coupling_ref.1) | copy-start | bytes 13828
  0.0 44.2 %copy-start.1 = (f32[6,8,768]{2,1,0:T(8,128)S(1)}, f32[6,8,768]{2,1,0:T(8,128)}, u32[]{:S(2)}) copy-start(f32[6,8,768]{2,1,0:T(8,128)} %param.12) | copy-start | bytes 442372
  0.0 44.2 %copy-start = (bf16[7,6,8,1152]{3,2,1,0:T(8,128)(2,1)S(1)}, bf16[7,6,8,1152]{3,2,1,0:T(8,128)(2,1)}, u32[]{:S(2)}) copy-start(bf16[7,6,8,1152]{3,2,1,0:T(8,128)(2,1)} %source_ref.1) | copy-start | bytes 2322436
  2.6 47.2 %all-to-all-start = ((bf16[64,16,128]{2,1,0:T(8,128)(2,1)}), bf16[64,16,128]{2,1,0:T(8,128)(2,1)}, u32[]{:S(2)}, u32[]{:S(2)}) async-start(bf16[64,16,128]{2,1,0:T(8,128)(2,1)} %get-tuple-element.20), calls=%async_computation | async-start | bytes 524288 | tf_op jit(solution)/shard_map/all_to_all | solution.py:443
  19.4 30.4 %collective-permute-start.1 = (bf16[56,1152]{1,0:T(8,128)(2,1)}, bf16[56,1152]{1,0:T(8,128)(2,1)}, u32[]{:S(2)}, u32[]{:S(2)}) collective-permute-start(bf16[56,1152]{1,0:T(8,128)(2,1)} %get-tuple-element.32), channel_id=1, source_target_pairs={{8,16},{24,32},{40,48},{56,64},{72,80},{88,96},{104,112},{120,128}... | collective-permute-start | bytes 387080 | tf_op jit(solution)/shard_map/ppermute | solution.py:445
  22.7 27.1 %collective-permute-start.3 = (bf16[56,1152]{1,0:T(8,128)(2,1)}, bf16[56,1152]{1,0:T(8,128)(2,1)}, u32[]{:S(2)}, u32[]{:S(2)}) collective-permute-start(bf16[56,1152]{1,0:T(8,128)(2,1)} %get-tuple-element.34), channel_id=1, source_target_pairs={{0,8},{16,24},{32,40},{48,56},{64,72},{80,88},{96,104},{112,120},{... | collective-permute-start | bytes 387080 | tf_op jit(solution)/shard_map/ppermute | solution.py:446
  31.7 18.1 %collective-permute-start = (bf16[48,1152]{1,0:T(8,128)(2,1)}, bf16[48,1152]{1,0:T(8,128)(2,1)}, u32[]{:S(2)}, u32[]{:S(2)}) collective-permute-start(bf16[48,1152]{1,0:T(8,128)(2,1)} %get-tuple-element.31), channel_id=1, source_target_pairs={{1,2},{3,4},{5,6},{2,1},{4,3},{6,5},{9,10},{11,12},{13,14},{10,9},... | collective-permute-start | bytes 331784 | tf_op jit(solution)/shard_map/ppermute | solution.py:444
  33.7 16.0 %collective-permute-start.2 = (bf16[48,1152]{1,0:T(8,128)(2,1)}, bf16[48,1152]{1,0:T(8,128)(2,1)}, u32[]{:S(2)}, u32[]{:S(2)}) collective-permute-start(bf16[48,1152]{1,0:T(8,128)(2,1)} %get-tuple-element.33), channel_id=1, source_target_pairs={{0,1},{2,3},{4,5},{6,7},{1,0},{3,2},{5,4},{7,6},{8,9},{10,11},{12,... | collective-permute-start | bytes 331784 | tf_op jit(solution)/shard_map/ppermute | solution.py:447
